TPU v7x, 512 devices: a whole 4x4x16 slice. The times are simulated.
512 devices in a mesh: coef: 8 (over y, x_lo), grid: 64 (over z, x_hi, core).
Axes of the slice: x: 4 (x_hi: 2, x_lo: 2; x = x_hi * 2 + x_lo), y: 4, z: 16, core: 2. Of those that a mesh axis runs over, the one named last changes fastest.
Arguments:
- basis_values: bfloat16 [40960, 2688], P('grid'), may hold values from -6 to 6
- occ_coef: bfloat16 [40960, 1024], P('grid', 'coef'), may hold values from -0.125 to 0.125
- listed_panels: int32 [64, 21], P('grid'), may hold values from 0 to 319, as said below
- centres: float32 [3, 40960], replicated, may hold values from 0 to 4
- point_weights: float32 [40960], P('grid'), may hold values from 0.25 to 4
Outputs:
- exchange_tiles: float32 [40960, 1024], P('grid', 'coef')
Inputs may be any that keep to these rules, and one draw needn't show every extreme that they name: `listed_panels`: the panels of one batch are distinct; panel p belongs to batch p // 5, and batch b names only panels of batches b - 4 to b + 4.
All inputs are finite; a program needn't handle non-finite values.
Results may differ from a plain program's by a relative error of at most 0.0085.
Values may be sent and summed in bfloat16 or wider, within the bound.
A program may use at most 64 MiB of HBM per device.

v0:
```python
import jax
import jax.numpy as jnp
from jax import lax
from jax.sharding import PartitionSpec as P

ORBITALS = 1024
PANEL_ROWS = 128
PANELS_DEV = 5
REACH = 4
LISTED = 21


def from_behind(block, axis, distance):
    devices = range(lax.axis_size(axis))
    route = [(i - distance, i) for i in devices if i - distance in devices]
    return lax.ppermute(block, axis, route)


def padded(block, sides, width):
    for axis, dim in sides:
        count = lax.axis_size(axis)
        forward = [(i, i + 1) for i in range(count - 1)]
        backward = [(target, source) for source, target in forward]
        low = lax.ppermute(
            lax.slice_in_dim(block, block.shape[dim] - width, None, axis=dim), axis, forward
        )
        high = lax.ppermute(lax.slice_in_dim(block, 0, width, axis=dim), axis, backward)
        block = jnp.concatenate([low, block, high], axis=dim)
    return block


def nearby(panels, offset):
    return from_behind(panels, "grid", -offset)


def send_back(contrib, offset):
    return from_behind(contrib.astype(jnp.bfloat16), "grid", offset).astype(contrib.dtype)


def shards(basis_values, occ_coef, listed_panels, centres, point_weights):
    width = occ_coef.shape[1]
    points = basis_values.shape[0]
    panels = occ_coef.reshape(PANELS_DEV, PANEL_ROWS, width)
    listed = listed_panels[0]
    batch = lax.axis_index("grid")
    pieces = {0: panels}
    for offset in range(-REACH, REACH + 1):
        if offset != 0:
            pieces[offset] = nearby(panels, offset)
    candidates = jnp.concatenate([pieces[offset] for offset in range(-REACH, REACH + 1)], 0)
    chosen = jnp.take(candidates, listed - (batch - REACH) * PANELS_DEV, axis=0)
    field = jnp.dot(
        basis_values, chosen.reshape(LISTED * PANEL_ROWS, width), preferred_element_type=jnp.float32
    ).astype(jnp.bfloat16)
    near = padded(field, (("grid", 0),), points)
    partial_value = lax.dot_general(
        field, near, (((1,), (1,)), ((), ())), preferred_element_type=jnp.float32
    )
    partial_value = partial_value / jnp.sqrt(jnp.float32(ORBITALS))
    density = lax.psum(partial_value.astype(jnp.bfloat16), "coef").astype(jnp.float32)
    anchor = jnp.zeros((), jnp.int32)
    start = batch * points
    padded_centres = jnp.pad(centres, ((0, 0), (points, points)))
    own_centres = lax.dynamic_slice(centres, (anchor, start), (3, points))
    near_centres = lax.dynamic_slice(padded_centres, (anchor, start), (3, 3 * points))
    distance = jnp.zeros((points, 3 * points), jnp.float32)
    for axis in range(3):
        gap = own_centres[axis][:, None] - near_centres[axis][None, :]
        distance = distance + gap * gap
    kernel = 1.0 / jnp.sqrt(distance + 0.25)
    mixed = (kernel * density).astype(jnp.bfloat16)
    exchanged = jnp.dot(mixed, near, preferred_element_type=jnp.float32)
    weighted = (exchanged * point_weights[:, None] / jnp.sqrt(jnp.float32(3 * points))).astype(
        jnp.bfloat16
    )
    tiles = lax.dot_general(
        basis_values, weighted, (((0,), (0,)), ((), ())), preferred_element_type=jnp.float32
    )
    tiles = (tiles / jnp.sqrt(jnp.float32(points))).reshape(LISTED, PANEL_ROWS, width)
    contribs = {}
    for offset in range(-REACH, REACH + 1):
        first_panel = (batch + offset) * PANELS_DEV
        select = (
            listed[None, :] == first_panel + jnp.arange(PANELS_DEV, dtype=jnp.int32)[:, None]
        ).astype(jnp.float32)
        contribs[offset] = jnp.einsum("js,sro->jro", select, tiles)
    total = contribs[0]
    for offset in range(-REACH, REACH + 1):
        if offset != 0:
            total = total + send_back(contribs[offset], offset)
    return total.reshape(PANELS_DEV * PANEL_ROWS, width)


def solution(mesh):
    placed = (P("grid", None), P("grid", "coef"), P("grid", None), P(), P("grid"))
    return jax.shard_map(
        shards, mesh=mesh, in_specs=placed, out_specs=P("grid", "coef"), check_vma=False
    )
```

profile of v0, /device:TPU:388, one launch (start us, length us, event | category | flops | bytes accessed | tf_op | source)
XLA Modules:
  0.0 277.5 jit_solution(35657123346483395)
XLA Ops:
  6.5 3.2 %collective-permute-start = (bf16[5,128,128]{2,1,0:T(8,128)(2,1)}, bf16[5,128,128]{2,1,0:T(8,128)(2,1)}, u32[]{:S(2)}, u32[]{:S(2)}) collective-permute-start(bf16[5,128,128]{2,1,0:T(8,128)(2,1)} %bitcast.62), channel_id=1, source_target_pairs={{0,4},{1,5},{2,6},{3,7},{4,8},{5,9},{6,10},{7,11},{8,12},{9,13},{1... | collective-permute-start | bytes 491528 | tf_op jit(solution)/shard_map/ppermute | solution.py:16
  9.7 2.0 collective-permute-start.1
  11.8 4.9 %collective-permute-start.2 = (bf16[5,128,128]{2,1,0:T(8,128)(2,1)}, bf16[5,128,128]{2,1,0:T(8,128)(2,1)}, u32[]{:S(2)}, u32[]{:S(2)}) collective-permute-start(bf16[5,128,128]{2,1,0:T(8,128)(2,1)} %bitcast.64), channel_id=1, source_target_pairs={{0,2},{1,3},{2,4},{3,5},{4,6},{5,7},{6,8},{7,9},{8,10},{9,11},{10,... | collective-permute-start | bytes 491528 | tf_op jit(solution)/shard_map/ppermute | solution.py:16
  16.7 1.9 collective-permute-start.3
  18.6 5.1 %collective-permute-start.4 = (bf16[5,128,128]{2,1,0:T(8,128)(2,1)}, bf16[5,128,128]{2,1,0:T(8,128)(2,1)}, u32[]{:S(2)}, u32[]{:S(2)}) collective-permute-start(bf16[5,128,128]{2,1,0:T(8,128)(2,1)} %bitcast.66), channel_id=1, source_target_pairs={{1,0},{2,1},{3,2},{4,3},{5,4},{6,5},{7,6},{8,7},{9,8},{10,9},{11,1... | collective-permute-start | bytes 491528 | tf_op jit(solution)/shard_map/ppermute | solution.py:16
  23.8 0.7 compare_and_fusion
  24.5 0.1 broadcast_bitcast_fusion
  24.6 0.7 fusion.92
  25.2 0.0 collective-permute-done
  25.2 4.5 %collective-permute-start.5 = (bf16[5,128,128]{2,1,0:T(8,128)(2,1)}, bf16[5,128,128]{2,1,0:T(8,128)(2,1)S(1)}, u32[]{:S(2)}, u32[]{:S(2)}) collective-permute-start(bf16[5,128,128]{2,1,0:T(8,128)(2,1)} %bitcast.67), channel_id=1, source_target_pairs={{2,0},{3,1},{4,2},{5,3},{6,4},{7,5},{8,6},{9,7},{10,8},{11,9},{12,... | collective-permute-start | bytes 491528 | tf_op jit(solution)/shard_map/ppermute | solution.py:16
  29.8 1.6 constant_dynamic-update-slice_fusion.8
  31.3 0.0 collective-permute-done.1
  31.3 1.9 collective-permute-start.6
  33.3 1.6 constant_dynamic-update-slice_fusion.7
  34.8 2.9 %collective-permute-start.7 = (bf16[5,128,128]{2,1,0:T(8,128)(2,1)}, bf16[5,128,128]{2,1,0:T(8,128)(2,1)S(1)}, u32[]{:S(2)}, u32[]{:S(2)}) collective-permute-start(bf16[5,128,128]{2,1,0:T(8,128)(2,1)} %bitcast.69), channel_id=1, source_target_pairs={{4,0},{5,1},{6,2},{7,3},{8,4},{9,5},{10,6},{11,7},{12,8},{13,9},{1... | collective-permute-start | bytes 491528 | tf_op jit(solution)/shard_map/ppermute | solution.py:16
  37.8 1.6 constant_dynamic-update-slice_fusion.6
  39.4 1.6 constant_dynamic-update-slice_fusion.5
  40.9 1.6 constant_dynamic-update-slice_fusion.4
  42.5 1.6 constant_dynamic-update-slice_fusion.3
  44.1 0.0 collective-permute-done.5
  44.1 0.7 constant_dynamic-update-slice_fusion.2
  44.8 0.0 collective-permute-done.6
  44.8 0.7 constant_dynamic-update-slice_fusion.1
  45.5 0.0 collective-permute-done.7
  45.5 0.7 constant_dynamic-update-slice_fusion
  46.2 2.9 %gather_fusion = bf16[21,128,128]{2,1,0:T(8,128)(2,1)} fusion(bf16[45,128,128]{2,1,0:T(8,128)(2,1)} %constant_dynamic-update-slice_fusion, s32[1024]{0:T(1024)S(1)} %pad_clamp_fusion), kind=kCustom, calls=%fused_computation | custom fusion | bytes 1376340 | tf_op jit(solution)/shard_map/jit(_take)/gather | solution.py:51
  49.1 2.4 bitcast_select_fusion
  51.4 1.1 convolution_convert_fusion
  52.6 0.0 copy-start.6
  52.6 4.4 %collective-permute-start.8 = (bf16[640,128]{0,1:T(8,128)(2,1)S(1)}, bf16[640,128]{0,1:T(8,128)(2,1)S(1)}, u32[]{:S(2)}, u32[]{:S(2)}) collective-permute-start(bf16[640,128]{0,1:T(8,128)(2,1)S(1)} %bitcast.58), channel_id=1, source_target_pairs={{0,1},{1,2},{2,3},{3,4},{4,5},{5,6},{6,7},{7,8},{8,9},{9,10},{10,1... | collective-permute-start | bytes 491528 | tf_op jit(solution)/shard_map/ppermute | solution.py:24
  57.0 2.9 %collective-permute-start.9 = (bf16[640,128]{0,1:T(8,128)(2,1)S(1)}, bf16[640,128]{0,1:T(8,128)(2,1)S(1)}, u32[]{:S(2)}, u32[]{:S(2)}) collective-permute-start(bf16[640,128]{0,1:T(8,128)(2,1)S(1)} %bitcast.59), channel_id=1, source_target_pairs={{1,0},{2,1},{3,2},{4,3},{5,4},{6,5},{7,6},{8,7},{9,8},{10,9},{11,1... | collective-permute-start | bytes 491528 | tf_op jit(solution)/shard_map/ppermute | solution.py:27
  60.0 1.1 collective-permute-done.8
  61.0 2.3 collective-permute-done.9
  63.3 0.7 copy-done.4
  64.0 2.3 multiply_convert_fusion.1
  66.3 0.0 all-reduce.3.cloned.1.call-update
  66.3 0.9 dynamic-slice_reduce_fusion.2
  67.3 1.0 fusion.49
  68.3 135.7 %all-reduce.3.cloned.1.call-done = bf16[640,1920]{1,0:T(8,128)(2,1)} async-done(((bf16[640,1920]{1,0:T(8,128)(2,1)}), bf16[640,1920]{1,0:T(8,128)(2,1)}) %all-reduce.3.cloned.1.call-update) | async-done | bytes 2457616 | tf_op jit(solution)/shard_map/psum | solution.py:60
  204.1 6.0 %fusion = bf16[2688,128]{0,1:T(8,128)(2,1)} fusion(bf16[640,2688]{1,0:T(8,128)(2,1)S(1)} %copy-done, bf16[640,1920]{1,0:T(8,128)(2,1)} %all-reduce.3.cloned.1.call-done, f32[1920]{0:T(1024)S(1)} %get-tuple-element.10, f32[640]{0:T(1024)S(1)} %get-tuple-element.7, f32[1920]{0:T(1024)S(1)} %get-tuple-element.9, f32[640]{0:T(1024)S(1)} %get-tuple-element.6, ...), kind=kOutput, calls=%fused_computation.4 | convolution fusion | flops 772128768 | bytes 7111168 | tf_op jit(solution)/shard_map/dot_general | solution.py:76
  210.1 2.2 copy.15
  212.3 1.8 fusion.20
  214.1 4.5 %collective-permute-start.10 = (bf16[5,128,128]{2,0,1:T(8,128)(2,1)S(1)}, bf16[5,128,128]{2,0,1:T(8,128)(2,1)}, u32[]{:S(2)}, u32[]{:S(2)}) collective-permute-start(bf16[5,128,128]{2,0,1:T(8,128)(2,1)S(1)} %fusion.20), channel_id=1, source_target_pairs={{4,0},{5,1},{6,2},{7,3},{8,4},{9,5},{10,6},{11,7},{12,8},{13,9},{1... | collective-permute-start | bytes 491528 | tf_op jit(solution)/shard_map/ppermute | solution.py:16
  218.6 1.7 fusion.23
  220.3 2.2 collective-permute-start.11
  222.5 1.7 fusion.26
  224.2 2.8 collective-permute-start.12
  227.0 1.4 fusion.29
  228.4 5.4 %collective-permute-start.13 = (bf16[5,128,128]{2,0,1:T(8,128)(2,1)}, bf16[5,128,128]{2,0,1:T(8,128)(2,1)}, u32[]{:S(2)}, u32[]{:S(2)}) collective-permute-start(bf16[5,128,128]{2,0,1:T(8,128)(2,1)} %fusion.29), channel_id=1, source_target_pairs={{1,0},{2,1},{3,2},{4,3},{5,4},{6,5},{7,6},{8,7},{9,8},{10,9},{11,1... | collective-permute-start | bytes 491528 | tf_op jit(solution)/shard_map/ppermute | solution.py:16
  233.8 1.3 fusion.32
  235.1 2.1 collective-permute-start.14
  237.2 1.3 fusion.35
  238.5 1.3 fusion.38
  239.9 1.3 fusion.41
  241.2 0.0 collective-permute-done.10
  241.2 5.5 %collective-permute-start.15 = (bf16[5,128,128]{2,0,1:T(8,128)(2,1)}, bf16[5,128,128]{2,0,1:T(8,128)(2,1)}, u32[]{:S(2)}, u32[]{:S(2)}) collective-permute-start(bf16[5,128,128]{2,0,1:T(8,128)(2,1)} %fusion.35), channel_id=1, source_target_pairs={{0,2},{1,3},{2,4},{3,5},{4,6},{5,7},{6,8},{7,9},{8,10},{9,11},{10,... | collective-permute-start | bytes 491528 | tf_op jit(solution)/shard_map/ppermute | solution.py:16
  246.7 5.0 %collective-permute-start.16 = (bf16[5,128,128]{2,0,1:T(8,128)(2,1)}, bf16[5,128,128]{2,0,1:T(8,128)(2,1)}, u32[]{:S(2)}, u32[]{:S(2)}) collective-permute-start(bf16[5,128,128]{2,0,1:T(8,128)(2,1)} %fusion.38), channel_id=1, source_target_pairs={{0,3},{1,4},{2,5},{3,6},{4,7},{5,8},{6,9},{7,10},{8,11},{9,12},{10... | collective-permute-start | bytes 491528 | tf_op jit(solution)/shard_map/ppermute | solution.py:16
  251.7 1.9 collective-permute-start.17
  253.6 0.0 collective-permute-done.14
  253.6 0.0 collective-permute-done.15
  253.6 7.6 %collective-permute-done.16 = bf16[5,128,128]{2,0,1:T(8,128)(2,1)} collective-permute-done((bf16[5,128,128]{2,0,1:T(8,128)(2,1)}, bf16[5,128,128]{2,0,1:T(8,128)(2,1)}, u32[]{:S(2)}, u32[]{:S(2)}) %collective-permute-start.16) | collective-permute-done | bytes 163872 | tf_op jit(solution)/shard_map/ppermute | solution.py:16
  261.2 6.1 %collective-permute-done.17 = bf16[5,128,128]{2,0,1:T(8,128)(2,1)} collective-permute-done((bf16[5,128,128]{2,0,1:T(8,128)(2,1)}, bf16[5,128,128]{2,0,1:T(8,128)(2,1)}, u32[]{:S(2)}, u32[]{:S(2)}) %collective-permute-start.17) | collective-permute-done | bytes 163872 | tf_op jit(solution)/shard_map/ppermute | solution.py:16
  267.4 2.5 convert_add_fusion
  269.9 0.8 copy.25
  (29 shorter events, 0.1 us)
Async XLA Ops:
  6.5 44.9 %copy-start = (bf16[640,2688]{1,0:T(8,128)(2,1)S(1)}, bf16[640,2688]{1,0:T(8,128)(2,1)}, u32[]{:S(2)}) copy-start(bf16[640,2688]{1,0:T(8,128)(2,1)} %param.5) | copy-start | bytes 10321924
  6.5 197.6 %all-reduce.3.cloned.1.call-start = ((), (), s32[]{:S(2)}) async-start(), calls=%async_computation | async-start | bytes 4915200 | tf_op jit(solution)/shard_map/psum | solution.py:60
  6.5 18.7 %collective-permute-start = (bf16[5,128,128]{2,1,0:T(8,128)(2,1)}, bf16[5,128,128]{2,1,0:T(8,128)(2,1)}, u32[]{:S(2)}, u32[]{:S(2)}) collective-permute-start(bf16[5,128,128]{2,1,0:T(8,128)(2,1)} %bitcast.62), channel_id=1, source_target_pairs={{0,4},{1,5},{2,6},{3,7},{4,8},{5,9},{6,10},{7,11},{8,12},{9,13},{1... | collective-permute-start | bytes 491528 | tf_op jit(solution)/shard_map/ppermute | solution.py:16
  9.7 21.6 %collective-permute-start.1 = (bf16[5,128,128]{2,1,0:T(8,128)(2,1)}, bf16[5,128,128]{2,1,0:T(8,128)(2,1)}, u32[]{:S(2)}, u32[]{:S(2)}) collective-permute-start(bf16[5,128,128]{2,1,0:T(8,128)(2,1)} %bitcast.63), channel_id=1, source_target_pairs={{0,3},{1,4},{2,5},{3,6},{4,7},{5,8},{6,9},{7,10},{8,11},{9,12},{10... | collective-permute-start | bytes 491528 | tf_op jit(solution)/shard_map/ppermute | solution.py:16
  11.8 23.1 %collective-permute-start.2 = (bf16[5,128,128]{2,1,0:T(8,128)(2,1)}, bf16[5,128,128]{2,1,0:T(8,128)(2,1)}, u32[]{:S(2)}, u32[]{:S(2)}) collective-permute-start(bf16[5,128,128]{2,1,0:T(8,128)(2,1)} %bitcast.64), channel_id=1, source_target_pairs={{0,2},{1,3},{2,4},{3,5},{4,6},{5,7},{6,8},{7,9},{8,10},{9,11},{10,... | collective-permute-start | bytes 491528 | tf_op jit(solution)/shard_map/ppermute | solution.py:16
  16.7 22.6 %collective-permute-start.3 = (bf16[5,128,128]{2,1,0:T(8,128)(2,1)}, bf16[5,128,128]{2,1,0:T(8,128)(2,1)}, u32[]{:S(2)}, u32[]{:S(2)}) collective-permute-start(bf16[5,128,128]{2,1,0:T(8,128)(2,1)} %bitcast.65), channel_id=1, source_target_pairs={{0,1},{1,2},{2,3},{3,4},{4,5},{5,6},{6,7},{7,8},{8,9},{9,10},{10,1... | collective-permute-start | bytes 491528 | tf_op jit(solution)/shard_map/ppermute | solution.py:16
  18.6 23.9 %collective-permute-start.4 = (bf16[5,128,128]{2,1,0:T(8,128)(2,1)}, bf16[5,128,128]{2,1,0:T(8,128)(2,1)}, u32[]{:S(2)}, u32[]{:S(2)}) collective-permute-start(bf16[5,128,128]{2,1,0:T(8,128)(2,1)} %bitcast.66), channel_id=1, source_target_pairs={{1,0},{2,1},{3,2},{4,3},{5,4},{6,5},{7,6},{8,7},{9,8},{10,9},{11,1... | collective-permute-start | bytes 491528 | tf_op jit(solution)/shard_map/ppermute | solution.py:16
  25.2 18.9 %collective-permute-start.5 = (bf16[5,128,128]{2,1,0:T(8,128)(2,1)}, bf16[5,128,128]{2,1,0:T(8,128)(2,1)S(1)}, u32[]{:S(2)}, u32[]{:S(2)}) collective-permute-start(bf16[5,128,128]{2,1,0:T(8,128)(2,1)} %bitcast.67), channel_id=1, source_target_pairs={{2,0},{3,1},{4,2},{5,3},{6,4},{7,5},{8,6},{9,7},{10,8},{11,9},{12,... | collective-permute-start | bytes 491528 | tf_op jit(solution)/shard_map/ppermute | solution.py:16
  31.3 13.5 %collective-permute-start.6 = (bf16[5,128,128]{2,1,0:T(8,128)(2,1)}, bf16[5,128,128]{2,1,0:T(8,128)(2,1)S(1)}, u32[]{:S(2)}, u32[]{:S(2)}) collective-permute-start(bf16[5,128,128]{2,1,0:T(8,128)(2,1)} %bitcast.68), channel_id=1, source_target_pairs={{3,0},{4,1},{5,2},{6,3},{7,4},{8,5},{9,6},{10,7},{11,8},{12,9},{13... | collective-permute-start | bytes 491528 | tf_op jit(solution)/shard_map/ppermute | solution.py:16
  34.8 10.6 %collective-permute-start.7 = (bf16[5,128,128]{2,1,0:T(8,128)(2,1)}, bf16[5,128,128]{2,1,0:T(8,128)(2,1)S(1)}, u32[]{:S(2)}, u32[]{:S(2)}) collective-permute-start(bf16[5,128,128]{2,1,0:T(8,128)(2,1)} %bitcast.69), channel_id=1, source_target_pairs={{4,0},{5,1},{6,2},{7,3},{8,4},{9,5},{10,6},{11,7},{12,8},{13,9},{1... | collective-permute-start | bytes 491528 | tf_op jit(solution)/shard_map/ppermute | solution.py:16
  52.6 10.7 %copy-start.2 = (bf16[128,640]{1,0:T(8,128)(2,1)}, bf16[128,640]{1,0:T(8,128)(2,1)S(1)}, u32[]{:S(2)}) copy-start(bf16[128,640]{1,0:T(8,128)(2,1)S(1)} %convolution_convert_fusion) | copy-start | bytes 491524
  52.6 151.5 %copy-start.6 = (f32[640]{0:T(1024)S(1)}, f32[640]{0:T(1024)}, u32[]{:S(2)}) copy-start(f32[640]{0:T(1024)} %param.9) | copy-start | bytes 7684
  52.6 8.4 %collective-permute-start.8 = (bf16[640,128]{0,1:T(8,128)(2,1)S(1)}, bf16[640,128]{0,1:T(8,128)(2,1)S(1)}, u32[]{:S(2)}, u32[]{:S(2)}) collective-permute-start(bf16[640,128]{0,1:T(8,128)(2,1)S(1)} %bitcast.58), channel_id=1, source_target_pairs={{0,1},{1,2},{2,3},{3,4},{4,5},{5,6},{6,7},{7,8},{8,9},{9,10},{10,1... | collective-permute-start | bytes 491528 | tf_op jit(solution)/shard_map/ppermute | solution.py:24
  57.0 6.3 %collective-permute-start.9 = (bf16[640,128]{0,1:T(8,128)(2,1)S(1)}, bf16[640,128]{0,1:T(8,128)(2,1)S(1)}, u32[]{:S(2)}, u32[]{:S(2)}) collective-permute-start(bf16[640,128]{0,1:T(8,128)(2,1)S(1)} %bitcast.59), channel_id=1, source_target_pairs={{1,0},{2,1},{3,2},{4,3},{5,4},{6,5},{7,6},{8,7},{9,8},{10,9},{11,1... | collective-permute-start | bytes 491528 | tf_op jit(solution)/shard_map/ppermute | solution.py:27
  61.0 2.3 copy-start.3
  63.3 0.7 copy-start.4
  204.1 8.2 %copy-start.5 = (s32[1,21]{1,0:T(1,128)S(1)}, s32[1,21]{1,0:T(1,128)}, u32[]{:S(2)}) copy-start(s32[1,21]{1,0:T(1,128)} %param.7) | copy-start | bytes 256
  212.3 14.7 %copy-start.1 = (bf16[2688,128]{1,0:T(8,128)(2,1)S(1)}, bf16[2688,128]{1,0:T(8,128)(2,1)}, u32[]{:S(2)}) copy-start(bf16[2688,128]{1,0:T(8,128)(2,1)} %copy.15) | copy-start | bytes 2064388
  214.1 27.1 %collective-permute-start.10 = (bf16[5,128,128]{2,0,1:T(8,128)(2,1)S(1)}, bf16[5,128,128]{2,0,1:T(8,128)(2,1)}, u32[]{:S(2)}, u32[]{:S(2)}) collective-permute-start(bf16[5,128,128]{2,0,1:T(8,128)(2,1)S(1)} %fusion.20), channel_id=1, source_target_pairs={{4,0},{5,1},{6,2},{7,3},{8,4},{9,5},{10,6},{11,7},{12,8},{13,9},{1... | collective-permute-start | bytes 491528 | tf_op jit(solution)/shard_map/ppermute | solution.py:16
  220.3 26.4 %collective-permute-start.11 = (bf16[5,128,128]{2,0,1:T(8,128)(2,1)S(1)}, bf16[5,128,128]{2,0,1:T(8,128)(2,1)}, u32[]{:S(2)}, u32[]{:S(2)}) collective-permute-start(bf16[5,128,128]{2,0,1:T(8,128)(2,1)S(1)} %fusion.23), channel_id=1, source_target_pairs={{3,0},{4,1},{5,2},{6,3},{7,4},{8,5},{9,6},{10,7},{11,8},{12,9},{13... | collective-permute-start | bytes 491528 | tf_op jit(solution)/shard_map/ppermute | solution.py:16
  224.2 27.4 %collective-permute-start.12 = (bf16[5,128,128]{2,0,1:T(8,128)(2,1)S(1)}, bf16[5,128,128]{2,0,1:T(8,128)(2,1)}, u32[]{:S(2)}, u32[]{:S(2)}) collective-permute-start(bf16[5,128,128]{2,0,1:T(8,128)(2,1)S(1)} %fusion.26), channel_id=1, source_target_pairs={{2,0},{3,1},{4,2},{5,3},{6,4},{7,5},{8,6},{9,7},{10,8},{11,9},{12,... | collective-permute-start | bytes 491528 | tf_op jit(solution)/shard_map/ppermute | solution.py:16
  228.4 25.2 %collective-permute-start.13 = (bf16[5,128,128]{2,0,1:T(8,128)(2,1)}, bf16[5,128,128]{2,0,1:T(8,128)(2,1)}, u32[]{:S(2)}, u32[]{:S(2)}) collective-permute-start(bf16[5,128,128]{2,0,1:T(8,128)(2,1)} %fusion.29), channel_id=1, source_target_pairs={{1,0},{2,1},{3,2},{4,3},{5,4},{6,5},{7,6},{8,7},{9,8},{10,9},{11,1... | collective-permute-start | bytes 491528 | tf_op jit(solution)/shard_map/ppermute | solution.py:16
  235.1 18.5 %collective-permute-start.14 = (bf16[5,128,128]{2,0,1:T(8,128)(2,1)}, bf16[5,128,128]{2,0,1:T(8,128)(2,1)}, u32[]{:S(2)}, u32[]{:S(2)}) collective-permute-start(bf16[5,128,128]{2,0,1:T(8,128)(2,1)} %fusion.32), channel_id=1, source_target_pairs={{0,1},{1,2},{2,3},{3,4},{4,5},{5,6},{6,7},{7,8},{8,9},{9,10},{10,1... | collective-permute-start | bytes 491528 | tf_op jit(solution)/shard_map/ppermute | solution.py:16
  241.2 12.4 %collective-permute-start.15 = (bf16[5,128,128]{2,0,1:T(8,128)(2,1)}, bf16[5,128,128]{2,0,1:T(8,128)(2,1)}, u32[]{:S(2)}, u32[]{:S(2)}) collective-permute-start(bf16[5,128,128]{2,0,1:T(8,128)(2,1)} %fusion.35), channel_id=1, source_target_pairs={{0,2},{1,3},{2,4},{3,5},{4,6},{5,7},{6,8},{7,9},{8,10},{9,11},{10,... | collective-permute-start | bytes 491528 | tf_op jit(solution)/shard_map/ppermute | solution.py:16
  246.7 14.5 %collective-permute-start.16 = (bf16[5,128,128]{2,0,1:T(8,128)(2,1)}, bf16[5,128,128]{2,0,1:T(8,128)(2,1)}, u32[]{:S(2)}, u32[]{:S(2)}) collective-permute-start(bf16[5,128,128]{2,0,1:T(8,128)(2,1)} %fusion.38), channel_id=1, source_target_pairs={{0,3},{1,4},{2,5},{3,6},{4,7},{5,8},{6,9},{7,10},{8,11},{9,12},{10... | collective-permute-start | bytes 491528 | tf_op jit(solution)/shard_map/ppermute | solution.py:16
  251.7 15.7 %collective-permute-start.17 = (bf16[5,128,128]{2,0,1:T(8,128)(2,1)}, bf16[5,128,128]{2,0,1:T(8,128)(2,1)}, u32[]{:S(2)}, u32[]{:S(2)}) collective-permute-start(bf16[5,128,128]{2,0,1:T(8,128)(2,1)} %fusion.41), channel_id=1, source_target_pairs={{0,4},{1,5},{2,6},{3,7},{4,8},{5,9},{6,10},{7,11},{8,12},{9,13},{1... | collective-permute-start | bytes 491528 | tf_op jit(solution)/shard_map/ppermute | solution.py:16
Sparse Core Ops, SparseCore 0:
  66.4 137.6 all-reduce.2
where the time goes:
time: 279 us; the launch traced here: 277 us
  waiting for transfers between devices  153 us (55%)
  starting transfers between devices  63.2 us (23%)
  matrix products  23.8 us (9%)
  local copies, waits for them, and re-layouts  20.1 us (7%)
  between operations  13.8 us (5%)
  other arithmetic  3.73 us (1%)
    psum x1, waiting for transfers between devices, shards(): lax.psum(partial_value.astype(jnp.bfloat16), 'coef').astype(jnp.float32)  136 us
    ppermute x16, starting transfers between devices, from_behind(): return lax.ppermute(block, axis, route)  55.9 us
    dot_general x9, matrix products, shards(): contribs[offset] = jnp.einsum('js,sro->jro', select, tiles)  14.4 us
    ppermute x16, waiting for transfers between devices, from_behind(): return lax.ppermute(block, axis, route)  13.8 us
    unnamed x22, local copies, waits for them, and re-layouts  11.6 us
    dot_general x1, matrix products, shards(): lax.dot_general(basis_values, weighted, (((0,), (0,)), ((), ())), preferr...  5.96 us
  transfers between devices with their start and end apart: 19, of which 5 were waited for; matrix products, arithmetic and copies ran while one was open for 9% of the time, Pallas kernels for 0%

commit v1 on v0

v1 whole, which is shorter than its diff:
```python
import functools
import math

import jax
import jax.numpy as jnp
from jax import lax
from jax.experimental import pallas as pl
from jax.experimental.pallas import tpu as pltpu
from jax.sharding import PartitionSpec as P

PANEL_ROWS = 128
PANELS_DEV = 5
LISTED = 21
PAIRS = (-2, -1, 1, 2)
ROW_PARTS = 2
MESH = pl.DeviceIdType.MESH


def fused(
    nc, ng, orbitals,
    basis_hbm, occ_hbm, listed, centres_hbm, weights_hbm, out_ref,
    basis, basis_t, cand, chosen, coords, columns, inverse, near_own, near_par,
    ext_rows, kern_own, kern_par, kern_ext, send_own, send_ext, got_own, got_ext,
    weighted, tiles, to_mate, from_mate, to_owner, from_owner,
    local_sem, occ_send, occ_recv, mate_send, mate_recv,
    field_send, field_recv, pass_send, pass_recv, ext_send, ext_recv,
    own_send, own_recv, back_send, back_recv,
    comb_send, comb_recv, final_send, final_recv,
):
    points, width = near_own.shape[1:]
    rows = points // nc
    part = points // ROW_PARTS
    c = lax.axis_index("coef")
    b = lax.axis_index("grid")
    k = lax.rem(b, 2)
    mate = b + 1 - 2 * k
    outer = lax.rem(b - 1 + 2 * k + ng, ng)

    def at(coef, grid):
        return {"coef": coef, "grid": grid}

    def pair(d):
        return lax.rem(b + 2 * d + ng, ng)

    def remote(src, dst, send, recv, to):
        return pltpu.make_async_remote_copy(
            src_ref=src, dst_ref=dst, send_sem=send, recv_sem=recv, device_id=to, device_id_type=MESH
        )

    def coef_of(j):
        return lax.rem(c + j, nc)

    loads = [
        pltpu.make_async_copy(basis_hbm, basis, local_sem.at[0]),
        pltpu.make_async_copy(occ_hbm, cand.at[pl.ds(PANELS_DEV * (4 + k), PANELS_DEV)], local_sem.at[1]),
        pltpu.make_async_copy(centres_hbm.at[:, pl.ds(pl.multiple_of(b * points, 128), points)], coords.at[0, pl.ds(0, 3)], local_sem.at[2]),
        pltpu.make_async_copy(centres_hbm.at[:, pl.ds(pl.multiple_of(mate * points, 128), points)], coords.at[1, pl.ds(0, 3)], local_sem.at[3]),
        pltpu.make_async_copy(centres_hbm.at[:, pl.ds(pl.multiple_of(outer * points, 128), points)], coords.at[2, pl.ds(0, 3)], local_sem.at[4]),
        pltpu.make_async_copy(weights_hbm, coords.at[0, pl.ds(3, 1)], local_sem.at[5]),
    ]
    coords[...] = jnp.zeros_like(coords)
    for load in loads:
        load.start()

    barrier = pltpu.get_barrier_semaphore()
    pl.semaphore_signal(barrier, inc=1, device_id=at(c, mate), device_id_type=MESH)
    for d in PAIRS:
        pl.semaphore_signal(barrier, inc=1, device_id=at(c, pair(d)), device_id_type=MESH)
    for j in range(1, nc):
        pl.semaphore_signal(barrier, inc=1, device_id=at(coef_of(j), b), device_id_type=MESH)
    for j in range(nc):
        pl.semaphore_signal(barrier, inc=1, device_id=at(coef_of(j), outer), device_id_type=MESH)
    pl.semaphore_wait(barrier, 2 * nc + len(PAIRS))

    def panel_slot(d, parity):
        return cand.at[pl.ds(PANELS_DEV * (4 + 2 * d + parity), PANELS_DEV)]

    panel_out = [
        remote(occ_hbm, panel_slot(-d, k), occ_send.at[i], occ_recv.at[i], at(c, pair(d)))
        for i, d in enumerate(PAIRS)
    ]
    for copy in panel_out:
        copy.start()
    panel_mate = remote(occ_hbm, panel_slot(0, k), mate_send.at[4], mate_recv.at[4], at(c, mate))
    panel_mate.start()

    for load in loads:
        load.wait()

    def turn(s, carry):
        at_s = pl.ds(pl.multiple_of(s * PANEL_ROWS, 128), PANEL_ROWS)
        for r in range(points // 128):
            basis_t[at_s, r * 128 : (r + 1) * 128] = basis[r * 128 : (r + 1) * 128, at_s].T
        return carry

    lax.fori_loop(0, LISTED, turn, 0)

    for i in (0, 2):
        columns[i] = coords[i].T

    def distances(left, right, out):
        mine = columns[left, pl.ds(pl.multiple_of(c * rows, 8), rows), :]
        total = None
        for axis in range(3):
            gap = mine[:, axis : axis + 1] - coords[right, axis : axis + 1, :]
            total = gap * gap if total is None else total + gap * gap
        out[...] = lax.rsqrt(total + 0.25) * (1.0 / math.sqrt(orbitals))

    distances(0, 0, kern_own)
    distances(0, 1, kern_par)
    distances(2, 0, kern_ext)

    first = (b - k - 4) * PANELS_DEV

    def invert(q, carry):
        slot = jnp.int32(LISTED)
        for s in range(LISTED):
            slot = jnp.where(listed[0, s] - first == q, s, slot)
        inverse[q] = slot
        return carry

    lax.fori_loop(0, 10 * PANELS_DEV, invert, 0)
    tiles[LISTED] = jnp.zeros_like(tiles[LISTED])

    panel_pass = [
        remote(panel_slot(d, k), panel_slot(d, k), mate_send.at[i], mate_recv.at[i], at(c, mate))
        for i, d in enumerate(PAIRS)
    ]
    for i in range(len(PAIRS)):
        arrived = len(PAIRS) - 1 - i
        panel_out[arrived].wait_recv()
        panel_pass[i].start()
    panel_mate.wait()
    for copy in panel_pass:
        copy.wait()
    for copy in panel_out:
        copy.wait_send()

    def choose(s, carry):
        chosen[pl.ds(pl.multiple_of(s * PANEL_ROWS, 128), PANEL_ROWS), :] = cand[jnp.clip(listed[0, s] - first, 0, 10 * PANELS_DEV - 1)]
        return carry

    lax.fori_loop(0, LISTED, choose, 0)

    def own_part(buffer, who, r):
        return buffer.at[who, pl.ds(r * part, part)]

    def field_copy(j, r):
        return remote(own_part(near_own, c, r), own_part(near_own, c, r), field_send.at[j, r], field_recv.at[j, r], at(coef_of(j), b))

    def pass_copy(j, r):
        who = coef_of(nc - j)
        return remote(own_part(near_own, who, r), own_part(near_par, who, r), pass_send.at[j, r], pass_recv.at[j, r], at(c, mate))

    for r in range(ROW_PARTS):
        near_own[c, r * part : (r + 1) * part] = jnp.dot(
            basis[r * part : (r + 1) * part], chosen[...], preferred_element_type=jnp.float32
        ).astype(jnp.bfloat16)

        def send(j, carry, r=r):
            field_copy(j, r).start()
            return carry

        lax.fori_loop(1, nc, send, 0)
        pass_copy(0, r).start()

    def ext_copy(j):
        to = coef_of(j)
        return remote(
            near_own.at[c, pl.ds(pl.multiple_of(to * rows, 16), rows)], ext_rows.at[c],
            ext_send.at[j], ext_recv.at[j], at(to, outer),
        )

    def send_ext_rows(j, carry):
        ext_copy(j).start()
        return carry

    lax.fori_loop(0, nc, send_ext_rows, 0)

    for r in range(ROW_PARTS):
        def forward(j, carry, r=r):
            field_copy(j, r).wait_recv()
            pass_copy(j, r).start()
            return carry

        lax.fori_loop(1, nc, forward, 0)

    def wait_ext(j, carry):
        ext_copy(j).wait()
        return carry

    lax.fori_loop(0, nc, wait_ext, 0)

    def side(ref, at_rows):
        return jnp.concatenate([ref[i, at_rows, :] for i in range(nc)], axis=1)

    def whole(ref):
        return jnp.concatenate([ref[i] for i in range(nc)], axis=1)

    my_rows = pl.ds(pl.multiple_of(c * rows, 16), rows)
    nt = (((1,), (1,)), ((), ()))
    left = side(near_own, my_rows)
    both = jnp.concatenate([left, whole(ext_rows)], axis=0)
    density = lax.dot_general(both, whole(near_own), nt, preferred_element_type=jnp.float32)
    mixed_own = (density[:rows] * kern_own[...]).astype(jnp.bfloat16)
    mixed_ext = (density[rows:] * kern_ext[...]).astype(jnp.bfloat16)
    mixed = jnp.concatenate([mixed_own, mixed_ext], axis=0)

    def ext_back(j):
        to = coef_of(j)
        return remote(send_ext.at[to], got_ext.at[c], back_send.at[j], back_recv.at[j], at(to, outer))

    def own_back(j):
        to = coef_of(j)
        return remote(send_own.at[to], got_own.at[c], own_send.at[j], own_recv.at[j], at(to, b))

    exchanged = jnp.dot(mixed, whole(near_own), preferred_element_type=jnp.float32)
    for i in range(nc):
        send_ext[i] = exchanged[rows:, i * width : (i + 1) * width].astype(jnp.bfloat16)

    def start_ext(j, carry):
        ext_back(j).start()
        return carry

    lax.fori_loop(0, nc, start_ext, 0)

    for r in range(ROW_PARTS):
        def take(j, carry, r=r):
            pass_copy(j, r).wait()
            return carry

        lax.fori_loop(0, nc, take, 0)
    density_par = lax.dot_general(left, whole(near_par), nt, preferred_element_type=jnp.float32)
    mixed_par = (density_par * kern_par[...]).astype(jnp.bfloat16)
    exchanged_own = exchanged[:rows] + jnp.dot(mixed_par, whole(near_par), preferred_element_type=jnp.float32)
    for i in range(nc):
        send_own[i] = exchanged_own[:, i * width : (i + 1) * width].astype(jnp.bfloat16)

    def start_own(j, carry):
        own_back(j).start()
        return carry

    lax.fori_loop(1, nc, start_own, 0)
    got_own[c] = send_own[c]

    def finish_field(j, carry):
        own_back(j).wait()
        for r in range(ROW_PARTS):
            field_copy(j, r).wait_send()
        return carry

    lax.fori_loop(1, nc, finish_field, 0)

    def finish_ext(j, carry):
        ext_back(j).wait()
        return carry

    lax.fori_loop(0, nc, finish_ext, 0)

    inside = jnp.logical_or(jnp.logical_and(k == 0, b > 0), jnp.logical_and(k == 1, b < ng - 1))
    for i in range(nc):
        total = got_own[i].astype(jnp.float32)
        beyond = got_ext[i].astype(jnp.float32)
        total = total + jnp.where(inside, beyond, jnp.zeros_like(beyond))
        at_i = slice(i * rows, (i + 1) * rows)
        weighted[at_i] = (total * columns[0, at_i, 3:4] * (1.0 / math.sqrt(3 * points))).astype(jnp.bfloat16)

    group = 3

    def tile(s, carry):
        value = jnp.dot(
            basis_t[pl.ds(pl.multiple_of(s * group * PANEL_ROWS, 128), group * PANEL_ROWS), :],
            weighted[...], preferred_element_type=jnp.float32,
        ) * (1.0 / math.sqrt(points))
        for i in range(group):
            tiles[s * group + i] = value[i * PANEL_ROWS : (i + 1) * PANEL_ROWS]
        return carry

    lax.fori_loop(0, LISTED // group, tile, 0)

    order = (-2, 2, -1, 1, 0)

    def comb_copy(i):
        return remote(to_mate.at[i], from_mate.at[i], comb_send.at[i], comb_recv.at[i], at(c, mate))

    for i, d in enumerate(order):
        def gather(j, carry, i=i, d=d):
            q = PANELS_DEV * (5 + 2 * d - k) + j
            to_mate[i, j] = tiles[inverse[q]].astype(jnp.bfloat16)
            return carry

        lax.fori_loop(0, PANELS_DEV, gather, 0)
        comb_copy(i).start()

    def final_copy(i):
        return remote(to_owner.at[i], from_owner.at[i], final_send.at[i], final_recv.at[i], at(c, pair(order[i])))

    for i, d in enumerate(order):
        comb_copy(i).wait()

        def combine(j, carry, i=i, d=d):
            q = PANELS_DEV * (4 + 2 * d + k) + j
            total = tiles[inverse[q]] + from_mate[i, j].astype(jnp.float32)
            if d == 0:
                out_ref[j] = total
            else:
                to_owner[i, j] = total.astype(jnp.bfloat16)
            return carry

        lax.fori_loop(0, PANELS_DEV, combine, 0)
        if d != 0:
            final_copy(i).start()
    for i in range(len(PAIRS)):
        final_copy(i).wait()
    for j in range(PANELS_DEV):
        total = out_ref[j]
        for i in range(len(PAIRS)):
            total = total + from_owner[i, j].astype(jnp.float32)
        out_ref[j] = total


def solution(mesh):
    nc, ng = mesh.shape["coef"], mesh.shape["grid"]

    def shards(basis_values, occ_coef, listed_panels, centres, point_weights):
        points, functions = basis_values.shape
        width = occ_coef.shape[1]
        rows = points // nc
        bf16, f32 = jnp.bfloat16, jnp.float32
        dma = pltpu.SemaphoreType.DMA
        panel = (PANEL_ROWS, width)
        anywhere = pl.BlockSpec(memory_space=pl.ANY)
        out = pl.pallas_call(
            functools.partial(fused, nc, ng, nc * width),
            out_shape=jax.ShapeDtypeStruct((PANELS_DEV, *panel), f32),
            in_specs=[anywhere, anywhere, pl.BlockSpec(memory_space=pltpu.SMEM), anywhere, anywhere],
            out_specs=pl.BlockSpec(memory_space=pltpu.VMEM),
            scratch_shapes=[
                pltpu.VMEM((points, functions), bf16),
                pltpu.VMEM((functions, points), bf16),
                pltpu.VMEM((10 * PANELS_DEV, *panel), bf16),
                pltpu.VMEM((functions, width), bf16),
                pltpu.VMEM((3, 8, points), f32),
                pltpu.VMEM((3, points, 8), f32),
                pltpu.SMEM((10 * PANELS_DEV,), jnp.int32),
                pltpu.VMEM((nc, points, width), bf16),
                pltpu.VMEM((nc, points, width), bf16),
                pltpu.VMEM((nc, rows, width), bf16),
                pltpu.VMEM((rows, points), f32),
                pltpu.VMEM((rows, points), f32),
                pltpu.VMEM((rows, points), f32),
                pltpu.VMEM((nc, rows, width), bf16),
                pltpu.VMEM((nc, rows, width), bf16),
                pltpu.VMEM((nc, rows, width), bf16),
                pltpu.VMEM((nc, rows, width), bf16),
                pltpu.VMEM((points, width), bf16),
                pltpu.VMEM((LISTED + 1, *panel), f32),
                pltpu.VMEM((5, PANELS_DEV, *panel), bf16),
                pltpu.VMEM((5, PANELS_DEV, *panel), bf16),
                pltpu.VMEM((4, PANELS_DEV, *panel), bf16),
                pltpu.VMEM((4, PANELS_DEV, *panel), bf16),
                dma((6,)),
                dma((4,)), dma((4,)), dma((5,)), dma((5,)),
                dma((nc, ROW_PARTS)), dma((nc, ROW_PARTS)),
                dma((nc, ROW_PARTS)), dma((nc, ROW_PARTS)),
                dma((nc,)), dma((nc,)),
                dma((nc,)), dma((nc,)), dma((nc,)), dma((nc,)),
                dma((5,)), dma((5,)), dma((4,)), dma((4,)),
            ],
            compiler_params=pltpu.CompilerParams(
                collective_id=0, has_side_effects=True, vmem_limit_bytes=56 * 2**20
            ),
        )(
            basis_values,
            occ_coef.reshape(PANELS_DEV, *panel),
            listed_panels,
            centres,
            point_weights.reshape(1, points),
        )
        return out.reshape(PANELS_DEV * PANEL_ROWS, width)

    placed = (P("grid", None), P("grid", "coef"), P("grid", None), P(), P("grid"))
    return jax.shard_map(
        shards, mesh=mesh, in_specs=placed, out_specs=P("grid", "coef"), check_vma=False
    )
```

time: 279 us -> 75.4 us (0.27)
  the two profiles are of different devices: /device:TPU:388 before, /device:TPU:1 now
where the time goes in v1:
time: 75.4 us; the launch traced here: 75.2 us
  Pallas kernels  72.2 us (96%)
  local copies, waits for them, and re-layouts  2.98 us (4%)
    pallas_call x1, Pallas kernels, shards(): pl.pallas_call(functools.partial(fused, nc, ng, nc * width), out_shape=ja...  72.2 us
    unnamed x1, local copies, waits for them, and re-layouts  1.72 us

profile of v1, /device:TPU:1, one launch (start us, length us, event | category | flops | bytes accessed | tf_op | source)
XLA Modules:
  0.0 75.2 jit_solution(14737880769286039618)
XLA Ops:
  0.0 1.3 %reshape.10.weights_hbm = f32[1,640]{1,0:T(1,128)} reshape(f32[640]{0:T(1024)} %param.9) | data formatting | bytes 5120 | tf_op jit(solution)/shard_map/reshape | solution.py:378
  1.3 72.2 %shard_map.55 = f32[5,128,128]{2,1,0:T(8,128)} custom-call(bf16[640,2688]{1,0:T(8,128)(2,1)} %basis_hbm.1, bf16[5,128,128]{2,1,0:T(8,128)(2,1)} %bitcast.3, s32[1,21]{1,0:T(1,128)} %listed.1, f32[3,40960]{1,0:T(4,128)} %centres_hbm.1, f32[1,640]{1,0:T(1,128)} %reshape.10.weights_hbm), custom_call_target="tpu_custom_call" | custom-call | tf_op jit(solution)/shard_map/pallas_call | solution.py:333
  73.5 1.7 %copy.7 = f32[640,128]{1,0:T(8,128)} copy(f32[640,128]{1,0:T(8,128)} %bitcast.2) | data formatting | bytes 655360

commit v2 on v1

--- a/solution.py
+++ b/solution.py
@@ -18,10 +18,10 @@
 
 def fused(
     nc, ng, orbitals,
-    basis_hbm, occ_hbm, listed, centres_hbm, weights_hbm, out_ref,
+    basis_hbm, occ_hbm, listed, centres_hbm, weights_hbm, out_ref, from_owner,
     basis, basis_t, cand, chosen, coords, columns, inverse, near_own, near_par,
     ext_rows, kern_own, kern_par, kern_ext, send_own, send_ext, got_own, got_ext,
-    weighted, tiles, to_mate, from_mate, to_owner, from_owner,
+    weighted, tiles, to_mate, from_mate, to_owner, line,
     local_sem, occ_send, occ_recv, mate_send, mate_recv,
     field_send, field_recv, pass_send, pass_recv, ext_send, ext_recv,
     own_send, own_recv, back_send, back_recv,
@@ -34,13 +34,17 @@
     b = lax.axis_index("grid")
     k = lax.rem(b, 2)
     mate = b + 1 - 2 * k
-    outer = lax.rem(b - 1 + 2 * k + ng, ng)
+    outer = b - 1 + 2 * k
+    inside = jnp.logical_and(outer >= 0, outer < ng)
 
     def at(coef, grid):
         return {"coef": coef, "grid": grid}
 
     def pair(d):
-        return lax.rem(b + 2 * d + ng, ng)
+        return b + 2 * d
+
+    def exists(d):
+        return pair(d) >= 0 if d < 0 else pair(d) < ng
 
     def remote(src, dst, send, recv, to):
         return pltpu.make_async_remote_copy(
@@ -49,28 +53,42 @@
 
     def coef_of(j):
         return lax.rem(c + j, nc)
+
+    barrier = pltpu.get_barrier_semaphore()
+    pl.semaphore_signal(barrier, inc=1, device_id=at(c, mate), device_id_type=MESH)
+    expected = jnp.int32(nc)
+    for d in PAIRS:
+        @pl.when(exists(d))
+        def _(d=d):
+            pl.semaphore_signal(barrier, inc=1, device_id=at(c, pair(d)), device_id_type=MESH)
+
+        expected += exists(d).astype(jnp.int32)
+    for j in range(1, nc):
+        pl.semaphore_signal(barrier, inc=1, device_id=at(coef_of(j), b), device_id_type=MESH)
+
+    @pl.when(inside)
+    def _():
+        for j in range(nc):
+            pl.semaphore_signal(barrier, inc=1, device_id=at(coef_of(j), outer), device_id_type=MESH)
+
+    expected += inside.astype(jnp.int32) * nc
 
     loads = [
         pltpu.make_async_copy(basis_hbm, basis, local_sem.at[0]),
         pltpu.make_async_copy(occ_hbm, cand.at[pl.ds(PANELS_DEV * (4 + k), PANELS_DEV)], local_sem.at[1]),
         pltpu.make_async_copy(centres_hbm.at[:, pl.ds(pl.multiple_of(b * points, 128), points)], coords.at[0, pl.ds(0, 3)], local_sem.at[2]),
         pltpu.make_async_copy(centres_hbm.at[:, pl.ds(pl.multiple_of(mate * points, 128), points)], coords.at[1, pl.ds(0, 3)], local_sem.at[3]),
-        pltpu.make_async_copy(centres_hbm.at[:, pl.ds(pl.multiple_of(outer * points, 128), points)], coords.at[2, pl.ds(0, 3)], local_sem.at[4]),
-        pltpu.make_async_copy(weights_hbm, coords.at[0, pl.ds(3, 1)], local_sem.at[5]),
+        pltpu.make_async_copy(weights_hbm, line, local_sem.at[4]),
     ]
     coords[...] = jnp.zeros_like(coords)
     for load in loads:
         load.start()
-
-    barrier = pltpu.get_barrier_semaphore()
-    pl.semaphore_signal(barrier, inc=1, device_id=at(c, mate), device_id_type=MESH)
-    for d in PAIRS:
-        pl.semaphore_signal(barrier, inc=1, device_id=at(c, pair(d)), device_id_type=MESH)
-    for j in range(1, nc):
-        pl.semaphore_signal(barrier, inc=1, device_id=at(coef_of(j), b), device_id_type=MESH)
-    for j in range(nc):
-        pl.semaphore_signal(barrier, inc=1, device_id=at(coef_of(j), outer), device_id_type=MESH)
-    pl.semaphore_wait(barrier, 2 * nc + len(PAIRS))
+    load_outer = pltpu.make_async_copy(
+        centres_hbm.at[:, pl.ds(pl.multiple_of(jnp.clip(outer, 0, ng - 1) * points, 128), points)], coords.at[2, pl.ds(0, 3)], local_sem.at[5]
+    )
+    load_outer.start()
+
+    pl.semaphore_wait(barrier, expected)
 
     def panel_slot(d, parity):
         return cand.at[pl.ds(PANELS_DEV * (4 + 2 * d + parity), PANELS_DEV)]
@@ -79,13 +97,15 @@
         remote(occ_hbm, panel_slot(-d, k), occ_send.at[i], occ_recv.at[i], at(c, pair(d)))
         for i, d in enumerate(PAIRS)
     ]
-    for copy in panel_out:
-        copy.start()
+    for copy, d in zip(panel_out, PAIRS):
+        pl.when(exists(d))(copy.start)
     panel_mate = remote(occ_hbm, panel_slot(0, k), mate_send.at[4], mate_recv.at[4], at(c, mate))
     panel_mate.start()
 
     for load in loads:
         load.wait()
+    load_outer.wait()
+    coords[0, 3:4] = line[...].reshape(1, points)
 
     def turn(s, carry):
         at_s = pl.ds(pl.multiple_of(s * PANEL_ROWS, 128), PANEL_ROWS)
@@ -126,15 +146,18 @@
         remote(panel_slot(d, k), panel_slot(d, k), mate_send.at[i], mate_recv.at[i], at(c, mate))
         for i, d in enumerate(PAIRS)
     ]
-    for i in range(len(PAIRS)):
-        arrived = len(PAIRS) - 1 - i
-        panel_out[arrived].wait_recv()
-        panel_pass[i].start()
+    for i, d in enumerate(PAIRS):
+        @pl.when(exists(d))
+        def _(i=i):
+            panel_out[len(PAIRS) - 1 - i].wait_recv()
+            panel_pass[i].start()
+
     panel_mate.wait()
-    for copy in panel_pass:
-        copy.wait()
-    for copy in panel_out:
-        copy.wait_send()
+    for i, d in enumerate(PAIRS):
+        @pl.when(exists(d))
+        def _(i=i):
+            panel_pass[i].wait()
+            panel_out[i].wait_send()
 
     def choose(s, carry):
         chosen[pl.ds(pl.multiple_of(s * PANEL_ROWS, 128), PANEL_ROWS), :] = cand[jnp.clip(listed[0, s] - first, 0, 10 * PANELS_DEV - 1)]
@@ -175,7 +198,9 @@
         ext_copy(j).start()
         return carry
 
-    lax.fori_loop(0, nc, send_ext_rows, 0)
+    @pl.when(inside)
+    def _():
+        lax.fori_loop(0, nc, send_ext_rows, 0)
 
     for r in range(ROW_PARTS):
         def forward(j, carry, r=r):
@@ -189,7 +214,9 @@
         ext_copy(j).wait()
         return carry
 
-    lax.fori_loop(0, nc, wait_ext, 0)
+    @pl.when(inside)
+    def _():
+        lax.fori_loop(0, nc, wait_ext, 0)
 
     def side(ref, at_rows):
         return jnp.concatenate([ref[i, at_rows, :] for i in range(nc)], axis=1)
@@ -222,7 +249,9 @@
         ext_back(j).start()
         return carry
 
-    lax.fori_loop(0, nc, start_ext, 0)
+    @pl.when(inside)
+    def _():
+        lax.fori_loop(0, nc, start_ext, 0)
 
     for r in range(ROW_PARTS):
         def take(j, carry, r=r):
@@ -255,9 +284,10 @@
         ext_back(j).wait()
         return carry
 
-    lax.fori_loop(0, nc, finish_ext, 0)
-
-    inside = jnp.logical_or(jnp.logical_and(k == 0, b > 0), jnp.logical_and(k == 1, b < ng - 1))
+    @pl.when(inside)
+    def _():
+        lax.fori_loop(0, nc, finish_ext, 0)
+
     for i in range(nc):
         total = got_own[i].astype(jnp.float32)
         beyond = got_ext[i].astype(jnp.float32)
@@ -309,14 +339,25 @@
 
         lax.fori_loop(0, PANELS_DEV, combine, 0)
         if d != 0:
-            final_copy(i).start()
+            pl.when(exists(d))(final_copy(i).start)
+
+    def no_sender(i):
+        return pltpu.make_async_copy(from_mate.at[i], from_owner.at[i], local_sem.at[i])
+
     for i in range(len(PAIRS)):
-        final_copy(i).wait()
-    for j in range(PANELS_DEV):
-        total = out_ref[j]
-        for i in range(len(PAIRS)):
-            total = total + from_owner[i, j].astype(jnp.float32)
-        out_ref[j] = total
+        @pl.when(exists(-order[i]))
+        def _(i=i):
+            final_copy(i).wait_recv()
+
+        @pl.when(jnp.logical_not(exists(-order[i])))
+        def _(i=i):
+            from_mate[i] = jnp.zeros_like(from_mate[i])
+            no_sender(i).start()
+            no_sender(i).wait()
+
+        @pl.when(exists(order[i]))
+        def _(i=i):
+            final_copy(i).wait_send()
 
 
 def solution(mesh):
@@ -330,11 +371,14 @@
         dma = pltpu.SemaphoreType.DMA
         panel = (PANEL_ROWS, width)
         anywhere = pl.BlockSpec(memory_space=pl.ANY)
-        out = pl.pallas_call(
+        own, others = pl.pallas_call(
             functools.partial(fused, nc, ng, nc * width),
-            out_shape=jax.ShapeDtypeStruct((PANELS_DEV, *panel), f32),
+            out_shape=(
+                jax.ShapeDtypeStruct((PANELS_DEV, *panel), f32),
+                jax.ShapeDtypeStruct((4, PANELS_DEV, *panel), bf16),
+            ),
             in_specs=[anywhere, anywhere, pl.BlockSpec(memory_space=pltpu.SMEM), anywhere, anywhere],
-            out_specs=pl.BlockSpec(memory_space=pltpu.VMEM),
+            out_specs=(pl.BlockSpec(memory_space=pltpu.VMEM), anywhere),
             scratch_shapes=[
                 pltpu.VMEM((points, functions), bf16),
                 pltpu.VMEM((functions, points), bf16),
@@ -358,7 +402,7 @@
                 pltpu.VMEM((5, PANELS_DEV, *panel), bf16),
                 pltpu.VMEM((5, PANELS_DEV, *panel), bf16),
                 pltpu.VMEM((4, PANELS_DEV, *panel), bf16),
-                pltpu.VMEM((4, PANELS_DEV, *panel), bf16),
+                pltpu.VMEM((points,), f32),
                 dma((6,)),
                 dma((4,)), dma((4,)), dma((5,)), dma((5,)),
                 dma((nc, ROW_PARTS)), dma((nc, ROW_PARTS)),
@@ -375,8 +419,11 @@
             occ_coef.reshape(PANELS_DEV, *panel),
             listed_panels,
             centres,
-            point_weights.reshape(1, points),
+            point_weights,
         )
+        out = own
+        for i in range(len(PAIRS)):
+            out = out + others[i].astype(f32)
         return out.reshape(PANELS_DEV * PANEL_ROWS, width)
 
     placed = (P("grid", None), P("grid", "coef"), P("grid", None), P(), P("grid"))

time: 75.4 us -> 66.8 us (0.89)
  the two profiles are of different devices: /device:TPU:1 before, /device:TPU:96 now
where the time goes in v2:
time: 66.8 us; the launch traced here: 66.6 us
  Pallas kernels  64.6 us (97%)
  other arithmetic  2.05 us (3%)
    pallas_call x1, Pallas kernels, shards(): pl.pallas_call(functools.partial(fused, nc, ng, nc * width), out_shape=(j...  64.6 us
    add x1, other arithmetic, shards(): out = out + others[i].astype(f32)  2.05 us

profile of v2, /device:TPU:96, one launch (start us, length us, event | category | flops | bytes accessed | tf_op | source)
XLA Modules:
  0.0 66.6 jit_solution(15574457482119676998)
XLA Ops:
  0.0 64.6 %shard_map.55 = (f32[5,128,128]{2,1,0:T(8,128)}, bf16[4,5,128,128]{3,2,1,0:T(8,128)(2,1)}) custom-call(bf16[640,2688]{1,0:T(8,128)(2,1)} %basis_hbm.1, bf16[5,128,128]{2,1,0:T(8,128)(2,1)} %bitcast.14, s32[1,21]{1,0:T(1,128)} %listed.1, f32[3,40960]{1,0:T(4,128)} %centres_hbm.1, f32[640]{0:T(1024)} %weights_hbm.1), custom_call_target="tpu_custom_call" | custom-call | tf_op jit(solution)/shard_map/pallas_call | solution.py:374
  64.6 2.0 %convert_add_fusion = f32[5,128,128]{2,1,0:T(8,128)} fusion(f32[5,128,128]{2,1,0:T(8,128)} %get-tuple-element.7, bf16[4,5,128,128]{3,2,1,0:T(8,128)(2,1)} %get-tuple-element.8), kind=kLoop, calls=%fused_computation | loop fusion | flops 655360 | bytes 1310720 | tf_op jit(solution)/shard_map/add | solution.py:426

commit v3 on v2

--- a/solution.py
+++ b/solution.py
@@ -20,7 +20,7 @@
     nc, ng, orbitals,
     basis_hbm, occ_hbm, listed, centres_hbm, weights_hbm, out_ref, from_owner,
     basis, basis_t, cand, chosen, coords, columns, inverse, near_own, near_par,
-    ext_rows, kern_own, kern_par, kern_ext, send_own, send_ext, got_own, got_ext,
+    ext_rows, density, density_par, exchanged, kern_own, kern_par, kern_ext, send_own, send_ext, got_own, got_ext,
     weighted, tiles, to_mate, from_mate, to_owner, line,
     local_sem, occ_send, occ_recv, mate_send, mate_recv,
     field_send, field_recv, pass_send, pass_recv, ext_send, ext_recv,
@@ -165,128 +165,155 @@
 
     lax.fori_loop(0, LISTED, choose, 0)
 
-    def own_part(buffer, who, r):
-        return buffer.at[who, pl.ds(r * part, part)]
-
-    def field_copy(j, r):
-        return remote(own_part(near_own, c, r), own_part(near_own, c, r), field_send.at[j, r], field_recv.at[j, r], at(coef_of(j), b))
-
-    def pass_copy(j, r):
-        who = coef_of(nc - j)
-        return remote(own_part(near_own, who, r), own_part(near_par, who, r), pass_send.at[j, r], pass_recv.at[j, r], at(c, mate))
+    across = c + 1 - 2 * lax.rem(c, 2)
+    up = lax.rem(c + 2, nc)
+    down = lax.rem(c + nc - 2, nc)
+    far = lax.rem(c + 4, nc)
+
+    def other(slab):
+        return slab + 1 - 2 * lax.rem(slab, 2)
+
+    arrives = (down, up, across, far, other(down), other(up), other(far), c)
+    leaves = (
+        ((c, up),) * 2, ((c, down),) * 2, ((c, across),) * 2, ((down, up), (up, down)),
+        ((across, up),) * 2, ((across, down),) * 2, ((far, across),) * 2,
+    )
+
+    def piece(buffer, slab, r):
+        return buffer.at[slab, pl.ds(r * part, part)]
+
+    def field_copy(kind, r):
+        slab, to = leaves[kind][r]
+        return remote(
+            piece(near_own, slab, r), piece(near_own, slab, r),
+            field_send.at[kind, r], field_recv.at[kind, r], at(to, b),
+        )
+
+    def pass_copy(kind, r):
+        slab = arrives[kind]
+        return remote(
+            piece(near_own, slab, r), piece(near_par, slab, r),
+            pass_send.at[kind, r], pass_recv.at[kind, r], at(c, mate),
+        )
+
+    my_rows = pl.ds(pl.multiple_of(c * rows, 16), rows)
+
+    def ext_copy(kind):
+        slab = arrives[kind]
+        return remote(near_own.at[slab, my_rows], ext_rows.at[slab], ext_send.at[kind], ext_recv.at[kind], at(c, outer))
+
+    def arrived(kind, r, forward=()):
+        field_copy(kind, r).wait_recv()
+        for onward in forward:
+            field_copy(onward, r).start()
+        pass_copy(kind, r).start()
+        if r == ROW_PARTS - 1:
+            pl.when(inside)(ext_copy(kind).start)
 
     for r in range(ROW_PARTS):
         near_own[c, r * part : (r + 1) * part] = jnp.dot(
             basis[r * part : (r + 1) * part], chosen[...], preferred_element_type=jnp.float32
         ).astype(jnp.bfloat16)
-
-        def send(j, carry, r=r):
-            field_copy(j, r).start()
-            return carry
-
-        lax.fori_loop(1, nc, send, 0)
-        pass_copy(0, r).start()
-
-    def ext_copy(j):
-        to = coef_of(j)
-        return remote(
-            near_own.at[c, pl.ds(pl.multiple_of(to * rows, 16), rows)], ext_rows.at[c],
-            ext_send.at[j], ext_recv.at[j], at(to, outer),
+        for kind in (2, 0, 1):
+            field_copy(kind, r).start()
+        pass_copy(7, r).start()
+    pl.when(inside)(ext_copy(7).start)
+
+    nt = (((1,), (1,)), ((), ()))
+
+    def beside(ref, slabs, at_rows=slice(None)):
+        return jnp.concatenate([ref[slab, at_rows, :] for slab in slabs], axis=1)
+
+    def add_own(kinds, begin=False):
+        @pl.when(inside)
+        def _():
+            for kind in kinds:
+                ext_copy(kind).wait()
+
+        slabs = [arrives[kind] for kind in kinds]
+        both = jnp.concatenate([beside(near_own, slabs, my_rows), beside(ext_rows, slabs)], axis=0)
+        term = lax.dot_general(both, beside(near_own, slabs), nt, preferred_element_type=jnp.float32)
+        density[...] = term if begin else density[...] + term
+
+    def add_par(kinds, begin=False):
+        for kind in kinds:
+            for r in range(ROW_PARTS):
+                pass_copy(kind, r).wait()
+        slabs = [arrives[kind] for kind in kinds]
+        term = lax.dot_general(
+            beside(near_own, slabs, my_rows), beside(near_par, slabs), nt, preferred_element_type=jnp.float32
         )
-
-    def send_ext_rows(j, carry):
-        ext_copy(j).start()
-        return carry
-
-    @pl.when(inside)
-    def _():
-        lax.fori_loop(0, nc, send_ext_rows, 0)
-
-    for r in range(ROW_PARTS):
-        def forward(j, carry, r=r):
-            field_copy(j, r).wait_recv()
-            pass_copy(j, r).start()
-            return carry
-
-        lax.fori_loop(1, nc, forward, 0)
-
-    def wait_ext(j, carry):
-        ext_copy(j).wait()
-        return carry
-
-    @pl.when(inside)
-    def _():
-        lax.fori_loop(0, nc, wait_ext, 0)
-
-    def side(ref, at_rows):
-        return jnp.concatenate([ref[i, at_rows, :] for i in range(nc)], axis=1)
-
-    def whole(ref):
-        return jnp.concatenate([ref[i] for i in range(nc)], axis=1)
-
-    my_rows = pl.ds(pl.multiple_of(c * rows, 16), rows)
-    nt = (((1,), (1,)), ((), ()))
-    left = side(near_own, my_rows)
-    both = jnp.concatenate([left, whole(ext_rows)], axis=0)
-    density = lax.dot_general(both, whole(near_own), nt, preferred_element_type=jnp.float32)
-    mixed_own = (density[:rows] * kern_own[...]).astype(jnp.bfloat16)
-    mixed_ext = (density[rows:] * kern_ext[...]).astype(jnp.bfloat16)
-    mixed = jnp.concatenate([mixed_own, mixed_ext], axis=0)
-
-    def ext_back(j):
-        to = coef_of(j)
-        return remote(send_ext.at[to], got_ext.at[c], back_send.at[j], back_recv.at[j], at(to, outer))
-
-    def own_back(j):
-        to = coef_of(j)
-        return remote(send_own.at[to], got_own.at[c], own_send.at[j], own_recv.at[j], at(to, b))
-
-    exchanged = jnp.dot(mixed, whole(near_own), preferred_element_type=jnp.float32)
-    for i in range(nc):
-        send_ext[i] = exchanged[rows:, i * width : (i + 1) * width].astype(jnp.bfloat16)
-
-    def start_ext(j, carry):
-        ext_back(j).start()
-        return carry
-
-    @pl.when(inside)
-    def _():
-        lax.fori_loop(0, nc, start_ext, 0)
-
-    for r in range(ROW_PARTS):
-        def take(j, carry, r=r):
-            pass_copy(j, r).wait()
-            return carry
-
-        lax.fori_loop(0, nc, take, 0)
-    density_par = lax.dot_general(left, whole(near_par), nt, preferred_element_type=jnp.float32)
-    mixed_par = (density_par * kern_par[...]).astype(jnp.bfloat16)
-    exchanged_own = exchanged[:rows] + jnp.dot(mixed_par, whole(near_par), preferred_element_type=jnp.float32)
-    for i in range(nc):
-        send_own[i] = exchanged_own[:, i * width : (i + 1) * width].astype(jnp.bfloat16)
-
-    def start_own(j, carry):
-        own_back(j).start()
-        return carry
-
-    lax.fori_loop(1, nc, start_own, 0)
+        density_par[...] = term if begin else density_par[...] + term
+
+    arrived(2, 0, (4, 5))
+    arrived(0, 0, (3,))
+    arrived(1, 0)
+    arrived(2, 1, (4, 5))
+    arrived(1, 1, (3,))
+    arrived(0, 1)
+    arrived(3, 0, (6,))
+    arrived(3, 1, (6,))
+    add_own((7, 2), True)
+    add_par((7, 2), True)
+    arrived(4, 0)
+    arrived(5, 0)
+    arrived(4, 1)
+    arrived(5, 1)
+    add_own((0, 4))
+    add_par((0, 4))
+    add_own((1, 5))
+    add_par((1, 5))
+    arrived(6, 0)
+    arrived(6, 1)
+    add_par((3, 6))
+    mixed_par = (density_par[...] * kern_par[...]).astype(jnp.bfloat16)
+
+    def two(i):
+        return (2 * i, 2 * i + 1)
+
+    def from_par(i, carry):
+        exchanged[i] = jnp.dot(mixed_par, beside(near_par, two(i)), preferred_element_type=jnp.float32)
+        return carry
+
+    lax.fori_loop(0, nc // 2, from_par, 0)
+    add_own((3, 6))
+    mixed = (density[...] * jnp.concatenate([kern_own[...], kern_ext[...]], axis=0)).astype(jnp.bfloat16)
+
+    def ext_back(i, slab):
+        return remote(send_ext.at[i], got_ext.at[slab], back_send.at[i], back_recv.at[slab], at(i, outer))
+
+    def own_back(i, slab):
+        return remote(send_own.at[i], got_own.at[slab], own_send.at[i], own_recv.at[slab], at(i, b))
+
+    def from_own(i, carry):
+        both = jnp.dot(mixed, beside(near_own, two(i)), preferred_element_type=jnp.float32)
+        mine = both[:rows] + exchanged[i]
+        for n, to in enumerate(two(i)):
+            columns_n = slice(n * width, (n + 1) * width)
+            send_ext[to] = both[rows:, columns_n].astype(jnp.bfloat16)
+            pl.when(inside)(ext_back(to, c).start)
+            send_own[to] = mine[:, columns_n].astype(jnp.bfloat16)
+            pl.when(to != c)(own_back(to, c).start)
+        return carry
+
+    lax.fori_loop(0, nc // 2, from_own, 0)
     got_own[c] = send_own[c]
 
-    def finish_field(j, carry):
-        own_back(j).wait()
+    def finish(i, carry):
+        @pl.when(i != c)
+        def _():
+            own_back(i, i).wait()
+
+        @pl.when(inside)
+        def _():
+            ext_back(i, i).wait()
+
+        return carry
+
+    lax.fori_loop(0, nc, finish, 0)
+    for kind in range(len(leaves)):
         for r in range(ROW_PARTS):
-            field_copy(j, r).wait_send()
-        return carry
-
-    lax.fori_loop(1, nc, finish_field, 0)
-
-    def finish_ext(j, carry):
-        ext_back(j).wait()
-        return carry
-
-    @pl.when(inside)
-    def _():
-        lax.fori_loop(0, nc, finish_ext, 0)
+            field_copy(kind, r).wait_send()
 
     for i in range(nc):
         total = got_own[i].astype(jnp.float32)
@@ -295,7 +322,7 @@
         at_i = slice(i * rows, (i + 1) * rows)
         weighted[at_i] = (total * columns[0, at_i, 3:4] * (1.0 / math.sqrt(3 * points))).astype(jnp.bfloat16)
 
-    group = 3
+    group = 7
 
     def tile(s, carry):
         value = jnp.dot(
@@ -390,6 +417,9 @@
                 pltpu.VMEM((nc, points, width), bf16),
                 pltpu.VMEM((nc, points, width), bf16),
                 pltpu.VMEM((nc, rows, width), bf16),
+                pltpu.VMEM((2 * rows, points), f32),
+                pltpu.VMEM((rows, points), f32),
+                pltpu.VMEM((nc // 2, rows, 2 * width), f32),
                 pltpu.VMEM((rows, points), f32),
                 pltpu.VMEM((rows, points), f32),
                 pltpu.VMEM((rows, points), f32),

time: 66.8 us -> 66.1 us (0.990)
  the two profiles are of different devices: /device:TPU:96 before, /device:TPU:100 now
where the time goes in v3:
time: 66.1 us; the launch traced here: 65.9 us
  Pallas kernels  63.9 us (97%)
  other arithmetic  2.05 us (3%)
    pallas_call x1, Pallas kernels, shards(): pl.pallas_call(functools.partial(fused, nc, ng, nc * width), out_shape=(j...  63.9 us
    add x1, other arithmetic, shards(): out = out + others[i].astype(f32)  2.05 us

profile of v3, /device:TPU:100, one launch (start us, length us, event | category | flops | bytes accessed | tf_op | source)
XLA Modules:
  0.0 65.9 jit_solution(14776733045244125090)
XLA Ops:
  0.0 63.9 %shard_map.55 = (f32[5,128,128]{2,1,0:T(8,128)}, bf16[4,5,128,128]{3,2,1,0:T(8,128)(2,1)}) custom-call(bf16[640,2688]{1,0:T(8,128)(2,1)} %basis_hbm.1, bf16[5,128,128]{2,1,0:T(8,128)(2,1)} %bitcast.14, s32[1,21]{1,0:T(1,128)} %listed.1, f32[3,40960]{1,0:T(4,128)} %centres_hbm.1, f32[640]{0:T(1024)} %weights_hbm.1), custom_call_target="tpu_custom_call" | custom-call | tf_op jit(solution)/shard_map/pallas_call | solution.py:401
  63.9 2.0 %convert_add_fusion = f32[5,128,128]{2,1,0:T(8,128)} fusion(f32[5,128,128]{2,1,0:T(8,128)} %get-tuple-element.7, bf16[4,5,128,128]{3,2,1,0:T(8,128)(2,1)} %get-tuple-element.8), kind=kLoop, calls=%fused_computation | loop fusion | flops 655360 | bytes 1310720 | tf_op jit(solution)/shard_map/add | solution.py:456

commit v4 on v3

--- a/solution.py
+++ b/solution.py
@@ -13,6 +13,7 @@
 LISTED = 21
 PAIRS = (-2, -1, 1, 2)
 ROW_PARTS = 2
+FAR = (3, 6)
 MESH = pl.DeviceIdType.MESH
 
 
@@ -21,7 +22,7 @@
     basis_hbm, occ_hbm, listed, centres_hbm, weights_hbm, out_ref, from_owner,
     basis, basis_t, cand, chosen, coords, columns, inverse, near_own, near_par,
     ext_rows, density, density_par, exchanged, kern_own, kern_par, kern_ext, send_own, send_ext, got_own, got_ext,
-    weighted, tiles, to_mate, from_mate, to_owner, line,
+    weighted, to_mate, from_mate, to_owner, line,
     local_sem, occ_send, occ_recv, mate_send, mate_recv,
     field_send, field_recv, pass_send, pass_recv, ext_send, ext_recv,
     own_send, own_recv, back_send, back_recv,
@@ -110,7 +111,7 @@
     def turn(s, carry):
         at_s = pl.ds(pl.multiple_of(s * PANEL_ROWS, 128), PANEL_ROWS)
         for r in range(points // 128):
-            basis_t[at_s, r * 128 : (r + 1) * 128] = basis[r * 128 : (r + 1) * 128, at_s].T
+            basis_t[s, :, r * 128 : (r + 1) * 128] = basis[r * 128 : (r + 1) * 128, at_s].T
         return carry
 
     lax.fori_loop(0, LISTED, turn, 0)
@@ -140,7 +141,7 @@
         return carry
 
     lax.fori_loop(0, 10 * PANELS_DEV, invert, 0)
-    tiles[LISTED] = jnp.zeros_like(tiles[LISTED])
+    basis_t[LISTED] = jnp.zeros_like(basis_t[LISTED])
 
     panel_pass = [
         remote(panel_slot(d, k), panel_slot(d, k), mate_send.at[i], mate_recv.at[i], at(c, mate))
@@ -199,6 +200,10 @@
     my_rows = pl.ds(pl.multiple_of(c * rows, 16), rows)
 
     def ext_copy(kind):
+        if kind in FAR:
+            to = arrives[kind]
+            to_rows = pl.ds(pl.multiple_of(to * rows, 16), rows)
+            return remote(near_own.at[c, to_rows], ext_rows.at[c], ext_send.at[kind], ext_recv.at[kind], at(to, outer))
         slab = arrives[kind]
         return remote(near_own.at[slab, my_rows], ext_rows.at[slab], ext_send.at[kind], ext_recv.at[kind], at(c, outer))
 
@@ -207,7 +212,7 @@
         for onward in forward:
             field_copy(onward, r).start()
         pass_copy(kind, r).start()
-        if r == ROW_PARTS - 1:
+        if r == ROW_PARTS - 1 and kind not in FAR:
             pl.when(inside)(ext_copy(kind).start)
 
     for r in range(ROW_PARTS):
@@ -217,7 +222,8 @@
         for kind in (2, 0, 1):
             field_copy(kind, r).start()
         pass_copy(7, r).start()
-    pl.when(inside)(ext_copy(7).start)
+    for kind in (*FAR, 7):
+        pl.when(inside)(ext_copy(kind).start)
 
     nt = (((1,), (1,)), ((), ()))
 
@@ -245,12 +251,12 @@
         )
         density_par[...] = term if begin else density_par[...] + term
 
-    arrived(2, 0, (4, 5))
     arrived(0, 0, (3,))
     arrived(1, 0)
-    arrived(2, 1, (4, 5))
+    arrived(2, 0, (4, 5))
     arrived(1, 1, (3,))
     arrived(0, 1)
+    arrived(2, 1, (4, 5))
     arrived(3, 0, (6,))
     arrived(3, 1, (6,))
     add_own((7, 2), True)
@@ -322,50 +328,41 @@
         at_i = slice(i * rows, (i + 1) * rows)
         weighted[at_i] = (total * columns[0, at_i, 3:4] * (1.0 / math.sqrt(3 * points))).astype(jnp.bfloat16)
 
-    group = 7
-
-    def tile(s, carry):
-        value = jnp.dot(
-            basis_t[pl.ds(pl.multiple_of(s * group * PANEL_ROWS, 128), group * PANEL_ROWS), :],
-            weighted[...], preferred_element_type=jnp.float32,
-        ) * (1.0 / math.sqrt(points))
-        for i in range(group):
-            tiles[s * group + i] = value[i * PANEL_ROWS : (i + 1) * PANEL_ROWS]
-        return carry
-
-    lax.fori_loop(0, LISTED // group, tile, 0)
-
     order = (-2, 2, -1, 1, 0)
+
+    def share(d, parity):
+        first_q = PANELS_DEV * (4 + 2 * d + parity)
+        left = jnp.concatenate(
+            [
+                basis_t[inverse[first_q + j]]
+                for j in range(PANELS_DEV)
+            ],
+            axis=0,
+        )
+        value = jnp.dot(left, weighted[...], preferred_element_type=jnp.float32)
+        return (value * (1.0 / math.sqrt(points))).reshape(PANELS_DEV, PANEL_ROWS, width)
 
     def comb_copy(i):
         return remote(to_mate.at[i], from_mate.at[i], comb_send.at[i], comb_recv.at[i], at(c, mate))
 
-    for i, d in enumerate(order):
-        def gather(j, carry, i=i, d=d):
-            q = PANELS_DEV * (5 + 2 * d - k) + j
-            to_mate[i, j] = tiles[inverse[q]].astype(jnp.bfloat16)
-            return carry
-
-        lax.fori_loop(0, PANELS_DEV, gather, 0)
-        comb_copy(i).start()
-
     def final_copy(i):
         return remote(to_owner.at[i], from_owner.at[i], final_send.at[i], final_recv.at[i], at(c, pair(order[i])))
 
+    def for_mate(i):
+        to_mate[i] = share(order[i], 1 - k).astype(jnp.bfloat16)
+        comb_copy(i).start()
+
+    for_mate(0)
     for i, d in enumerate(order):
+        out_ref[...] = share(d, k)
+        if i + 1 < len(order):
+            for_mate(i + 1)
         comb_copy(i).wait()
-
-        def combine(j, carry, i=i, d=d):
-            q = PANELS_DEV * (4 + 2 * d + k) + j
-            total = tiles[inverse[q]] + from_mate[i, j].astype(jnp.float32)
-            if d == 0:
-                out_ref[j] = total
-            else:
-                to_owner[i, j] = total.astype(jnp.bfloat16)
-            return carry
-
-        lax.fori_loop(0, PANELS_DEV, combine, 0)
-        if d != 0:
+        total = out_ref[...] + from_mate[i].astype(jnp.float32)
+        if d == 0:
+            out_ref[...] = total
+        else:
+            to_owner[i] = total.astype(jnp.bfloat16)
             pl.when(exists(d))(final_copy(i).start)
 
     def no_sender(i):
@@ -408,7 +405,7 @@
             out_specs=(pl.BlockSpec(memory_space=pltpu.VMEM), anywhere),
             scratch_shapes=[
                 pltpu.VMEM((points, functions), bf16),
-                pltpu.VMEM((functions, points), bf16),
+                pltpu.VMEM((LISTED + 1, PANEL_ROWS, points), bf16),
                 pltpu.VMEM((10 * PANELS_DEV, *panel), bf16),
                 pltpu.VMEM((functions, width), bf16),
                 pltpu.VMEM((3, 8, points), f32),
@@ -428,7 +425,6 @@
                 pltpu.VMEM((nc, rows, width), bf16),
                 pltpu.VMEM((nc, rows, width), bf16),
                 pltpu.VMEM((points, width), bf16),
-                pltpu.VMEM((LISTED + 1, *panel), f32),
                 pltpu.VMEM((5, PANELS_DEV, *panel), bf16),
                 pltpu.VMEM((5, PANELS_DEV, *panel), bf16),
                 pltpu.VMEM((4, PANELS_DEV, *panel), bf16),

time: 66.1 us -> 64.3 us (0.973)
  the two profiles are of different devices: /device:TPU:100 before, /device:TPU:96 now
where the time goes in v4:
time: 64.3 us; the launch traced here: 64.1 us
  Pallas kernels  62.1 us (97%)
  other arithmetic  2.05 us (3%)
    pallas_call x1, Pallas kernels, shards(): pl.pallas_call(functools.partial(fused, nc, ng, nc * width), out_shape=(j...  62.1 us
    add x1, other arithmetic, shards(): out = out + others[i].astype(f32)  2.05 us

profile of v4, /device:TPU:96, one launch (start us, length us, event | category | flops | bytes accessed | tf_op | source)
XLA Modules:
  0.0 64.1 jit_solution(16185695981231344656)
XLA Ops:
  0.0 62.1 %shard_map.55 = (f32[5,128,128]{2,1,0:T(8,128)}, bf16[4,5,128,128]{3,2,1,0:T(8,128)(2,1)}) custom-call(bf16[640,2688]{1,0:T(8,128)(2,1)} %basis_hbm.1, bf16[5,128,128]{2,1,0:T(8,128)(2,1)} %bitcast.14, s32[1,21]{1,0:T(1,128)} %listed.1, f32[3,40960]{1,0:T(4,128)} %centres_hbm.1, f32[640]{0:T(1024)} %weights_hbm.1), custom_call_target="tpu_custom_call" | custom-call | tf_op jit(solution)/shard_map/pallas_call | solution.py:398
  62.1 2.0 %convert_add_fusion = f32[5,128,128]{2,1,0:T(8,128)} fusion(f32[5,128,128]{2,1,0:T(8,128)} %get-tuple-element.7, bf16[4,5,128,128]{3,2,1,0:T(8,128)(2,1)} %get-tuple-element.8), kind=kLoop, calls=%fused_computation | loop fusion | flops 655360 | bytes 1310720 | tf_op jit(solution)/shard_map/add | solution.py:452

commit v5 on v3

--- a/solution.py
+++ b/solution.py
@@ -12,16 +12,16 @@
 PANELS_DEV = 5
 LISTED = 21
 PAIRS = (-2, -1, 1, 2)
-ROW_PARTS = 2
+ROW_PARTS = 4
 MESH = pl.DeviceIdType.MESH
 
 
 def fused(
     nc, ng, orbitals,
-    basis_hbm, occ_hbm, listed, centres_hbm, weights_hbm, out_ref, from_owner,
-    basis, basis_t, cand, chosen, coords, columns, inverse, near_own, near_par,
-    ext_rows, density, density_par, exchanged, kern_own, kern_par, kern_ext, send_own, send_ext, got_own, got_ext,
-    weighted, tiles, to_mate, from_mate, to_owner, line,
+    basis_hbm, occ_hbm, listed, centres_hbm, weights_hbm, out_ref,
+    basis, cand, chosen, coords, columns, inverse, near_own, near_par,
+    ext_rows, exchanged, kern_own, kern_par, kern_ext, send_own, send_ext, got_own, got_ext,
+    weighted, tiles, to_mate, from_mate, to_owner, from_owner, line,
     local_sem, occ_send, occ_recv, mate_send, mate_recv,
     field_send, field_recv, pass_send, pass_recv, ext_send, ext_recv,
     own_send, own_recv, back_send, back_recv,
@@ -107,14 +107,6 @@
     load_outer.wait()
     coords[0, 3:4] = line[...].reshape(1, points)
 
-    def turn(s, carry):
-        at_s = pl.ds(pl.multiple_of(s * PANEL_ROWS, 128), PANEL_ROWS)
-        for r in range(points // 128):
-            basis_t[at_s, r * 128 : (r + 1) * 128] = basis[r * 128 : (r + 1) * 128, at_s].T
-        return carry
-
-    lax.fori_loop(0, LISTED, turn, 0)
-
     for i in (0, 2):
         columns[i] = coords[i].T
 
@@ -175,15 +167,14 @@
 
     arrives = (down, up, across, far, other(down), other(up), other(far), c)
     leaves = (
-        ((c, up),) * 2, ((c, down),) * 2, ((c, across),) * 2, ((down, up), (up, down)),
-        ((across, up),) * 2, ((across, down),) * 2, ((far, across),) * 2,
+        (c, up), (c, down), (c, across), None, (across, up), (across, down), (far, across),
     )
 
     def piece(buffer, slab, r):
         return buffer.at[slab, pl.ds(r * part, part)]
 
     def field_copy(kind, r):
-        slab, to = leaves[kind][r]
+        slab, to = leaves[kind] or ((down, up) if r % 2 == 0 else (up, down))
         return remote(
             piece(near_own, slab, r), piece(near_own, slab, r),
             field_send.at[kind, r], field_recv.at[kind, r], at(to, b),
@@ -198,17 +189,18 @@
 
     my_rows = pl.ds(pl.multiple_of(c * rows, 16), rows)
 
+    holders = (up, down, across, far, other(up), other(down), other(far), c)
+
     def ext_copy(kind):
-        slab = arrives[kind]
-        return remote(near_own.at[slab, my_rows], ext_rows.at[slab], ext_send.at[kind], ext_recv.at[kind], at(c, outer))
+        to = holders[kind]
+        to_rows = pl.ds(pl.multiple_of(to * rows, 16), rows)
+        return remote(near_own.at[c, to_rows], ext_rows.at[c], ext_send.at[kind], ext_recv.at[kind], at(to, outer))
 
     def arrived(kind, r, forward=()):
         field_copy(kind, r).wait_recv()
         for onward in forward:
             field_copy(onward, r).start()
         pass_copy(kind, r).start()
-        if r == ROW_PARTS - 1:
-            pl.when(inside)(ext_copy(kind).start)
 
     for r in range(ROW_PARTS):
         near_own[c, r * part : (r + 1) * part] = jnp.dot(
@@ -217,67 +209,40 @@
         for kind in (2, 0, 1):
             field_copy(kind, r).start()
         pass_copy(7, r).start()
-    pl.when(inside)(ext_copy(7).start)
+    for kind in range(nc):
+        pl.when(inside)(ext_copy(kind).start)
+
+    parts = range(ROW_PARTS)
+    for r in parts:
+        arrived(0, r, (3,) if r % 2 == 0 else ())
+        arrived(1, r, (3,) if r % 2 == 1 else ())
+    for r in parts:
+        arrived(2, r, (4, 5))
+    for r in parts:
+        arrived(3, r, (6,))
+    for r in parts:
+        arrived(4, r)
+        arrived(5, r)
+    for r in parts:
+        arrived(6, r)
 
     nt = (((1,), (1,)), ((), ()))
 
     def beside(ref, slabs, at_rows=slice(None)):
         return jnp.concatenate([ref[slab, at_rows, :] for slab in slabs], axis=1)
 
-    def add_own(kinds, begin=False):
-        @pl.when(inside)
-        def _():
-            for kind in kinds:
-                ext_copy(kind).wait()
-
-        slabs = [arrives[kind] for kind in kinds]
-        both = jnp.concatenate([beside(near_own, slabs, my_rows), beside(ext_rows, slabs)], axis=0)
-        term = lax.dot_general(both, beside(near_own, slabs), nt, preferred_element_type=jnp.float32)
-        density[...] = term if begin else density[...] + term
-
-    def add_par(kinds, begin=False):
-        for kind in kinds:
-            for r in range(ROW_PARTS):
-                pass_copy(kind, r).wait()
-        slabs = [arrives[kind] for kind in kinds]
-        term = lax.dot_general(
-            beside(near_own, slabs, my_rows), beside(near_par, slabs), nt, preferred_element_type=jnp.float32
-        )
-        density_par[...] = term if begin else density_par[...] + term
-
-    arrived(2, 0, (4, 5))
-    arrived(0, 0, (3,))
-    arrived(1, 0)
-    arrived(2, 1, (4, 5))
-    arrived(1, 1, (3,))
-    arrived(0, 1)
-    arrived(3, 0, (6,))
-    arrived(3, 1, (6,))
-    add_own((7, 2), True)
-    add_par((7, 2), True)
-    arrived(4, 0)
-    arrived(5, 0)
-    arrived(4, 1)
-    arrived(5, 1)
-    add_own((0, 4))
-    add_par((0, 4))
-    add_own((1, 5))
-    add_par((1, 5))
-    arrived(6, 0)
-    arrived(6, 1)
-    add_par((3, 6))
-    mixed_par = (density_par[...] * kern_par[...]).astype(jnp.bfloat16)
-
     def two(i):
         return (2 * i, 2 * i + 1)
 
-    def from_par(i, carry):
-        exchanged[i] = jnp.dot(mixed_par, beside(near_par, two(i)), preferred_element_type=jnp.float32)
-        return carry
-
-    lax.fori_loop(0, nc // 2, from_par, 0)
-    add_own((3, 6))
-    mixed = (density[...] * jnp.concatenate([kern_own[...], kern_ext[...]], axis=0)).astype(jnp.bfloat16)
+    @pl.when(inside)
+    def _():
+        for kind in range(nc):
+            ext_copy(kind).wait()
+
+    mine = beside(near_own, range(nc), my_rows)
+    both = jnp.concatenate([mine, beside(ext_rows, range(nc))], axis=0)
+    density = lax.dot_general(both, beside(near_own, range(nc)), nt, preferred_element_type=jnp.float32)
+    mixed = (density * jnp.concatenate([kern_own[...], kern_ext[...]], axis=0)).astype(jnp.bfloat16)
 
     def ext_back(i, slab):
         return remote(send_ext.at[i], got_ext.at[slab], back_send.at[i], back_recv.at[slab], at(i, outer))
@@ -286,17 +251,31 @@
         return remote(send_own.at[i], got_own.at[slab], own_send.at[i], own_recv.at[slab], at(i, b))
 
     def from_own(i, carry):
-        both = jnp.dot(mixed, beside(near_own, two(i)), preferred_element_type=jnp.float32)
-        mine = both[:rows] + exchanged[i]
+        value = jnp.dot(mixed, beside(near_own, two(i)), preferred_element_type=jnp.float32)
+        exchanged[i] = value[:rows]
         for n, to in enumerate(two(i)):
-            columns_n = slice(n * width, (n + 1) * width)
-            send_ext[to] = both[rows:, columns_n].astype(jnp.bfloat16)
+            send_ext[to] = value[rows:, n * width : (n + 1) * width].astype(jnp.bfloat16)
             pl.when(inside)(ext_back(to, c).start)
-            send_own[to] = mine[:, columns_n].astype(jnp.bfloat16)
+        return carry
+
+    lax.fori_loop(0, nc // 2, from_own, 0)
+
+    for kind in range(nc):
+        for r in parts:
+            pass_copy(kind, r).wait()
+    density_par = lax.dot_general(
+        beside(near_own, range(nc), my_rows), beside(near_par, range(nc)), nt, preferred_element_type=jnp.float32
+    )
+    mixed_par = (density_par * kern_par[...]).astype(jnp.bfloat16)
+
+    def from_par(i, carry):
+        value = exchanged[i] + jnp.dot(mixed_par, beside(near_par, two(i)), preferred_element_type=jnp.float32)
+        for n, to in enumerate(two(i)):
+            send_own[to] = value[:, n * width : (n + 1) * width].astype(jnp.bfloat16)
             pl.when(to != c)(own_back(to, c).start)
         return carry
 
-    lax.fori_loop(0, nc // 2, from_own, 0)
+    lax.fori_loop(0, nc // 2, from_par, 0)
     got_own[c] = send_own[c]
 
     def finish(i, carry):
@@ -322,69 +301,48 @@
         at_i = slice(i * rows, (i + 1) * rows)
         weighted[at_i] = (total * columns[0, at_i, 3:4] * (1.0 / math.sqrt(3 * points))).astype(jnp.bfloat16)
 
-    group = 7
-
-    def tile(s, carry):
+    turned = jnp.concatenate([weighted[i * 128 : (i + 1) * 128, :].T for i in range(points // 128)], axis=1)
+    group = 3
+    for s in range(LISTED // group):
         value = jnp.dot(
-            basis_t[pl.ds(pl.multiple_of(s * group * PANEL_ROWS, 128), group * PANEL_ROWS), :],
-            weighted[...], preferred_element_type=jnp.float32,
+            turned, basis[:, s * group * PANEL_ROWS : (s + 1) * group * PANEL_ROWS], preferred_element_type=jnp.float32
         ) * (1.0 / math.sqrt(points))
         for i in range(group):
-            tiles[s * group + i] = value[i * PANEL_ROWS : (i + 1) * PANEL_ROWS]
-        return carry
-
-    lax.fori_loop(0, LISTED // group, tile, 0)
-
-    order = (-2, 2, -1, 1, 0)
+            tiles[s * group + i] = value[:, i * PANEL_ROWS : (i + 1) * PANEL_ROWS]
+
+    order = (-1, 1, -2, 2, 0)
 
     def comb_copy(i):
         return remote(to_mate.at[i], from_mate.at[i], comb_send.at[i], comb_recv.at[i], at(c, mate))
 
-    for i, d in enumerate(order):
-        def gather(j, carry, i=i, d=d):
-            q = PANELS_DEV * (5 + 2 * d - k) + j
-            to_mate[i, j] = tiles[inverse[q]].astype(jnp.bfloat16)
-            return carry
-
-        lax.fori_loop(0, PANELS_DEV, gather, 0)
-        comb_copy(i).start()
-
     def final_copy(i):
         return remote(to_owner.at[i], from_owner.at[i], final_send.at[i], final_recv.at[i], at(c, pair(order[i])))
 
     for i, d in enumerate(order):
+        for j in range(PANELS_DEV):
+            to_mate[i, j] = tiles[inverse[PANELS_DEV * (5 + 2 * d - k) + j]].astype(jnp.bfloat16)
+        comb_copy(i).start()
+    for i, d in enumerate(order):
         comb_copy(i).wait()
-
-        def combine(j, carry, i=i, d=d):
-            q = PANELS_DEV * (4 + 2 * d + k) + j
-            total = tiles[inverse[q]] + from_mate[i, j].astype(jnp.float32)
+        for j in range(PANELS_DEV):
+            total = tiles[inverse[PANELS_DEV * (4 + 2 * d + k) + j]] + from_mate[i, j].astype(jnp.float32)
             if d == 0:
                 out_ref[j] = total
             else:
                 to_owner[i, j] = total.astype(jnp.bfloat16)
-            return carry
-
-        lax.fori_loop(0, PANELS_DEV, combine, 0)
         if d != 0:
             pl.when(exists(d))(final_copy(i).start)
 
-    def no_sender(i):
-        return pltpu.make_async_copy(from_mate.at[i], from_owner.at[i], local_sem.at[i])
-
-    for i in range(len(PAIRS)):
-        @pl.when(exists(-order[i]))
-        def _(i=i):
-            final_copy(i).wait_recv()
-
-        @pl.when(jnp.logical_not(exists(-order[i])))
-        def _(i=i):
-            from_mate[i] = jnp.zeros_like(from_mate[i])
-            no_sender(i).start()
-            no_sender(i).wait()
-
-        @pl.when(exists(order[i]))
-        def _(i=i):
-            final_copy(i).wait_send()
+    for i, d in enumerate(order[:-1]):
+        sent = exists(-d)
+        pl.when(sent)(final_copy(i).wait_recv)
+        for j in range(PANELS_DEV):
+            term = from_owner[i, j].astype(jnp.float32)
+            out_ref[j] += jnp.where(sent, term, jnp.zeros_like(term))
+    for j in range(PANELS_DEV):
+        out_ref[j] = out_ref[j].T
+    for i, d in enumerate(order[:-1]):
+        pl.when(exists(d))(final_copy(i).wait_send)
 
 
 def solution(mesh):
@@ -398,17 +356,13 @@
         dma = pltpu.SemaphoreType.DMA
         panel = (PANEL_ROWS, width)
         anywhere = pl.BlockSpec(memory_space=pl.ANY)
-        own, others = pl.pallas_call(
+        out = pl.pallas_call(
             functools.partial(fused, nc, ng, nc * width),
-            out_shape=(
-                jax.ShapeDtypeStruct((PANELS_DEV, *panel), f32),
-                jax.ShapeDtypeStruct((4, PANELS_DEV, *panel), bf16),
-            ),
+            out_shape=jax.ShapeDtypeStruct((PANELS_DEV, *panel), f32),
             in_specs=[anywhere, anywhere, pl.BlockSpec(memory_space=pltpu.SMEM), anywhere, anywhere],
-            out_specs=(pl.BlockSpec(memory_space=pltpu.VMEM), anywhere),
+            out_specs=pl.BlockSpec(memory_space=pltpu.VMEM),
             scratch_shapes=[
                 pltpu.VMEM((points, functions), bf16),
-                pltpu.VMEM((functions, points), bf16),
                 pltpu.VMEM((10 * PANELS_DEV, *panel), bf16),
                 pltpu.VMEM((functions, width), bf16),
                 pltpu.VMEM((3, 8, points), f32),
@@ -417,8 +371,6 @@
                 pltpu.VMEM((nc, points, width), bf16),
                 pltpu.VMEM((nc, points, width), bf16),
                 pltpu.VMEM((nc, rows, width), bf16),
-                pltpu.VMEM((2 * rows, points), f32),
-                pltpu.VMEM((rows, points), f32),
                 pltpu.VMEM((nc // 2, rows, 2 * width), f32),
                 pltpu.VMEM((rows, points), f32),
                 pltpu.VMEM((rows, points), f32),
@@ -431,6 +383,7 @@
                 pltpu.VMEM((LISTED + 1, *panel), f32),
                 pltpu.VMEM((5, PANELS_DEV, *panel), bf16),
                 pltpu.VMEM((5, PANELS_DEV, *panel), bf16),
+                pltpu.VMEM((4, PANELS_DEV, *panel), bf16),
                 pltpu.VMEM((4, PANELS_DEV, *panel), bf16),
                 pltpu.VMEM((points,), f32),
                 dma((6,)),
@@ -451,9 +404,6 @@
             centres,
             point_weights,
         )
-        out = own
-        for i in range(len(PAIRS)):
-            out = out + others[i].astype(f32)
         return out.reshape(PANELS_DEV * PANEL_ROWS, width)
 
     placed = (P("grid", None), P("grid", "coef"), P("grid", None), P(), P("grid"))

time: 66.1 us -> 59.3 us (0.90)
  the two profiles are of different devices: /device:TPU:100 before, /device:TPU:96 now
where the time goes in v5:
time: 59.3 us; the launch traced here: 59.1 us
  Pallas kernels  57.4 us (97%)
  local copies, waits for them, and re-layouts  1.72 us (3%)
    pallas_call x1, Pallas kernels, shards(): pl.pallas_call(functools.partial(fused, nc, ng, nc * width), out_shape=ja...  57.4 us
    unnamed x1, local copies, waits for them, and re-layouts  1.72 us

profile of v5, /device:TPU:96, one launch (start us, length us, event | category | flops | bytes accessed | tf_op | source)
XLA Modules:
  0.0 59.1 jit_solution(8428319538119569691)
XLA Ops:
  0.0 57.4 %shard_map.55 = f32[5,128,128]{2,1,0:T(8,128)} custom-call(bf16[640,2688]{1,0:T(8,128)(2,1)} %basis_hbm.1, bf16[5,128,128]{2,1,0:T(8,128)(2,1)} %bitcast.3, s32[1,21]{1,0:T(1,128)} %listed.1, f32[3,40960]{1,0:T(4,128)} %centres_hbm.1, f32[640]{0:T(1024)} %weights_hbm.1), custom_call_target="tpu_custom_call" | custom-call | tf_op jit(solution)/shard_map/pallas_call | solution.py:359
  57.4 1.7 %copy.7 = f32[640,128]{1,0:T(8,128)} copy(f32[640,128]{1,0:T(8,128)} %bitcast.2) | data formatting | bytes 655360

commit v6 on v5

--- a/solution.py
+++ b/solution.py
@@ -13,6 +13,7 @@
 LISTED = 21
 PAIRS = (-2, -1, 1, 2)
 ROW_PARTS = 4
+SPLIT = 2
 MESH = pl.DeviceIdType.MESH
 
 
@@ -44,7 +45,12 @@
         return b + 2 * d
 
     def exists(d):
-        return pair(d) >= 0 if d < 0 else pair(d) < ng
+        return jnp.logical_and(pair(d) >= 0, pair(d) < ng)
+
+    side = 1 - 2 * lax.rem(lax.div(b, 2), 2)
+    same, ahead, behind, diagonal = side, 2 * side, -2 * side, -side
+    has_ahead, has_behind = exists(ahead), exists(behind)
+    two_parts = ((0, SPLIT), (SPLIT, PANELS_DEV - SPLIT))
 
     def remote(src, dst, send, recv, to):
         return pltpu.make_async_remote_copy(
@@ -90,16 +96,42 @@
 
     pl.semaphore_wait(barrier, expected)
 
-    def panel_slot(d, parity):
-        return cand.at[pl.ds(PANELS_DEV * (4 + 2 * d + parity), PANELS_DEV)]
-
-    panel_out = [
-        remote(occ_hbm, panel_slot(-d, k), occ_send.at[i], occ_recv.at[i], at(c, pair(d)))
-        for i, d in enumerate(PAIRS)
-    ]
-    for copy, d in zip(panel_out, PAIRS):
-        pl.when(exists(d))(copy.start)
-    panel_mate = remote(occ_hbm, panel_slot(0, k), mate_send.at[4], mate_recv.at[4], at(c, mate))
+    def panel_slot(d, h):
+        start, size = two_parts[h]
+        return cand.at[pl.ds(PANELS_DEV * (4 + 2 * d + k) + start, size)]
+
+    def panel_copy(role, h):
+        start, size = two_parts[h]
+        mine = occ_hbm.at[pl.ds(start, size)]
+        src, to, dst = (
+            (mine, same, -same),
+            (mine, behind, ahead),
+            (mine, ahead, behind),
+            (panel_slot(same, h), ahead, diagonal) if h == 0 else (panel_slot(ahead, h), same, same),
+        )[role]
+        return remote(src, panel_slot(dst, h), occ_send.at[role, h], occ_recv.at[role, h], at(c, pair(to)))
+
+    arrives_from = (same, ahead, behind, diagonal)
+
+    def panel_pass(role, h):
+        slot = panel_slot(arrives_from[role], h)
+        return remote(slot, slot, mate_send.at[role, h], mate_recv.at[role, h], at(c, mate))
+
+    panel_copy(0, 0).start()
+
+    @pl.when(has_behind)
+    def _():
+        panel_copy(1, 1).start()
+        panel_copy(1, 0).start()
+
+    @pl.when(has_ahead)
+    def _():
+        panel_copy(2, 1).start()
+        panel_copy(2, 0).start()
+
+    panel_copy(0, 1).start()
+    whole_slot = cand.at[pl.ds(PANELS_DEV * (4 + k), PANELS_DEV)]
+    panel_mate = remote(occ_hbm, whole_slot, mate_send.at[4, 0], mate_recv.at[4, 0], at(c, mate))
     panel_mate.start()
 
     for load in loads:
@@ -134,22 +166,44 @@
     lax.fori_loop(0, 10 * PANELS_DEV, invert, 0)
     tiles[LISTED] = jnp.zeros_like(tiles[LISTED])
 
-    panel_pass = [
-        remote(panel_slot(d, k), panel_slot(d, k), mate_send.at[i], mate_recv.at[i], at(c, mate))
-        for i, d in enumerate(PAIRS)
-    ]
-    for i, d in enumerate(PAIRS):
-        @pl.when(exists(d))
-        def _(i=i):
-            panel_out[len(PAIRS) - 1 - i].wait_recv()
-            panel_pass[i].start()
+    def panel_here(role, h):
+        panel_copy(role, h).wait_recv()
+        panel_pass(role, h).start()
+
+    panel_here(0, 0)
+
+    @pl.when(has_ahead)
+    def _():
+        panel_copy(3, 0).start()
+        panel_here(1, 1)
+        panel_copy(3, 1).start()
+
+    pl.when(has_behind)(lambda: panel_here(2, 1))
+    panel_here(0, 1)
+    pl.when(has_ahead)(lambda: panel_here(1, 0))
+
+    @pl.when(has_behind)
+    def _():
+        panel_here(2, 0)
+        panel_here(3, 0)
+        panel_here(3, 1)
 
     panel_mate.wait()
-    for i, d in enumerate(PAIRS):
-        @pl.when(exists(d))
-        def _(i=i):
-            panel_pass[i].wait()
-            panel_out[i].wait_send()
+    for h in range(2):
+        panel_pass(0, h).wait()
+        panel_copy(0, h).wait_send()
+
+        @pl.when(has_ahead)
+        def _(h=h):
+            panel_pass(1, h).wait()
+            panel_copy(2, h).wait_send()
+            panel_copy(3, h).wait_send()
+
+        @pl.when(has_behind)
+        def _(h=h):
+            panel_pass(2, h).wait()
+            panel_pass(3, h).wait()
+            panel_copy(1, h).wait_send()
 
     def choose(s, carry):
         chosen[pl.ds(pl.multiple_of(s * PANEL_ROWS, 128), PANEL_ROWS), :] = cand[jnp.clip(listed[0, s] - first, 0, 10 * PANELS_DEV - 1)]
@@ -310,39 +364,85 @@
         for i in range(group):
             tiles[s * group + i] = value[:, i * PANEL_ROWS : (i + 1) * PANEL_ROWS]
 
-    order = (-1, 1, -2, 2, 0)
+    order = (diagonal, same, ahead, behind, 0)
+    DIAGONAL, SAME, AHEAD, BEHIND, HERE = range(5)
 
     def comb_copy(i):
         return remote(to_mate.at[i], from_mate.at[i], comb_send.at[i], comb_recv.at[i], at(c, mate))
 
-    def final_copy(i):
-        return remote(to_owner.at[i], from_owner.at[i], final_send.at[i], final_recv.at[i], at(c, pair(order[i])))
+    def part_of(buffer, i, h):
+        start, size = two_parts[h]
+        return buffer.at[i, pl.ds(start, size)]
+
+    def final_copy(i, h):
+        to = (behind, same)[h] if i == DIAGONAL else order[i]
+        return remote(
+            part_of(to_owner, i, h), part_of(from_owner, i, h), final_send.at[i, h], final_recv.at[i, h], at(c, pair(to))
+        )
+
+    def combine(i, h, merge=False):
+        start, size = two_parts[h]
+        for j in range(start, start + size):
+            total = tiles[inverse[PANELS_DEV * (4 + 2 * order[i] + k) + j]] + from_mate[i, j].astype(jnp.float32)
+            if merge:
+                term = from_owner[DIAGONAL, j].astype(jnp.float32)
+                total = total + jnp.where(has_ahead, term, jnp.zeros_like(term))
+            if i == HERE:
+                out_ref[j] = total
+            else:
+                to_owner[i, j] = total.astype(jnp.bfloat16)
 
     for i, d in enumerate(order):
         for j in range(PANELS_DEV):
             to_mate[i, j] = tiles[inverse[PANELS_DEV * (5 + 2 * d - k) + j]].astype(jnp.bfloat16)
         comb_copy(i).start()
-    for i, d in enumerate(order):
-        comb_copy(i).wait()
-        for j in range(PANELS_DEV):
-            total = tiles[inverse[PANELS_DEV * (4 + 2 * d + k) + j]] + from_mate[i, j].astype(jnp.float32)
-            if d == 0:
-                out_ref[j] = total
+
+    comb_copy(DIAGONAL).wait()
+    for h in (1, 0):
+        combine(DIAGONAL, h)
+        pl.when(has_behind)(final_copy(DIAGONAL, h).start)
+    comb_copy(SAME).wait()
+    combine(SAME, 1)
+    final_copy(SAME, 1).start()
+    comb_copy(AHEAD).wait()
+    combine(AHEAD, 0)
+    pl.when(has_ahead)(final_copy(AHEAD, 0).start)
+    comb_copy(BEHIND).wait()
+    for h in range(2):
+        combine(BEHIND, h)
+        pl.when(has_behind)(final_copy(BEHIND, h).start)
+    comb_copy(HERE).wait()
+    for h in range(2):
+        combine(HERE, h)
+    pl.when(has_ahead)(final_copy(DIAGONAL, 0).wait_recv)
+    combine(SAME, 0, merge=True)
+    final_copy(SAME, 0).start()
+
+    @pl.when(has_ahead)
+    def _():
+        final_copy(DIAGONAL, 1).wait_recv()
+        combine(AHEAD, 1, merge=True)
+        final_copy(AHEAD, 1).start()
+
+    for i, sent in ((BEHIND, has_ahead), (SAME, None), (AHEAD, has_behind)):
+        for h in range(2):
+            if sent is None:
+                final_copy(i, h).wait_recv()
             else:
-                to_owner[i, j] = total.astype(jnp.bfloat16)
-        if d != 0:
-            pl.when(exists(d))(final_copy(i).start)
-
-    for i, d in enumerate(order[:-1]):
-        sent = exists(-d)
-        pl.when(sent)(final_copy(i).wait_recv)
+                pl.when(sent)(final_copy(i, h).wait_recv)
         for j in range(PANELS_DEV):
             term = from_owner[i, j].astype(jnp.float32)
-            out_ref[j] += jnp.where(sent, term, jnp.zeros_like(term))
+            out_ref[j] += term if sent is None else jnp.where(sent, term, jnp.zeros_like(term))
     for j in range(PANELS_DEV):
         out_ref[j] = out_ref[j].T
-    for i, d in enumerate(order[:-1]):
-        pl.when(exists(d))(final_copy(i).wait_send)
+    for h in range(2):
+        final_copy(SAME, h).wait_send()
+        pl.when(has_ahead)(final_copy(AHEAD, h).wait_send)
+
+        @pl.when(has_behind)
+        def _(h=h):
+            final_copy(DIAGONAL, h).wait_send()
+            final_copy(BEHIND, h).wait_send()
 
 
 def solution(mesh):
@@ -387,12 +487,12 @@
                 pltpu.VMEM((4, PANELS_DEV, *panel), bf16),
                 pltpu.VMEM((points,), f32),
                 dma((6,)),
-                dma((4,)), dma((4,)), dma((5,)), dma((5,)),
+                dma((4, 2)), dma((4, 2)), dma((5, 2)), dma((5, 2)),
                 dma((nc, ROW_PARTS)), dma((nc, ROW_PARTS)),
                 dma((nc, ROW_PARTS)), dma((nc, ROW_PARTS)),
                 dma((nc,)), dma((nc,)),
                 dma((nc,)), dma((nc,)), dma((nc,)), dma((nc,)),
-                dma((5,)), dma((5,)), dma((4,)), dma((4,)),
+                dma((5,)), dma((5,)), dma((4, 2)), dma((4, 2)),
             ],
             compiler_params=pltpu.CompilerParams(
                 collective_id=0, has_side_effects=True, vmem_limit_bytes=56 * 2**20

time: 59.3 us -> 57.4 us (0.968)
  Pallas kernels: 57.4 us -> 55.6 us
    pallas_call x1, Pallas kernels: 57.4 us -> 55.6 us  [shards(): pl.pallas_call(functools.partial(fused, nc, ng, nc * width), out_shape=ja...]
where the time goes in v6:
time: 57.4 us; the launch traced here: 57.3 us
  Pallas kernels  55.6 us (97%)
  local copies, waits for them, and re-layouts  1.72 us (3%)
    pallas_call x1, Pallas kernels, shards(): pl.pallas_call(functools.partial(fused, nc, ng, nc * width), out_shape=ja...  55.6 us
    unnamed x1, local copies, waits for them, and re-layouts  1.72 us

profile of v6, /device:TPU:96, one launch (start us, length us, event | category | flops | bytes accessed | tf_op | source)
XLA Modules:
  0.0 57.3 jit_solution(15609976222119711532)
XLA Ops:
  0.0 55.6 %shard_map.55 = f32[5,128,128]{2,1,0:T(8,128)} custom-call(bf16[640,2688]{1,0:T(8,128)(2,1)} %basis_hbm.1, bf16[5,128,128]{2,1,0:T(8,128)(2,1)} %bitcast.3, s32[1,21]{1,0:T(1,128)} %listed.1, f32[3,40960]{1,0:T(4,128)} %centres_hbm.1, f32[640]{0:T(1024)} %weights_hbm.1), custom_call_target="tpu_custom_call" | custom-call | tf_op jit(solution)/shard_map/pallas_call | solution.py:459
  55.6 1.7 %copy.7 = f32[640,128]{1,0:T(8,128)} copy(f32[640,128]{1,0:T(8,128)} %bitcast.2) | data formatting | bytes 655360

commit v7 on v6

--- a/solution.py
+++ b/solution.py
@@ -13,14 +13,14 @@
 LISTED = 21
 PAIRS = (-2, -1, 1, 2)
 ROW_PARTS = 4
-SPLIT = 2
+SPLIT = 3
 MESH = pl.DeviceIdType.MESH
 
 
 def fused(
     nc, ng, orbitals,
-    basis_hbm, occ_hbm, listed, centres_hbm, weights_hbm, out_ref,
-    basis, cand, chosen, coords, columns, inverse, near_own, near_par,
+    basis_hbm, occ_hbm, listed_hbm, centres_hbm, weights_hbm, out_hbm,
+    listed, out_ref, basis, cand, chosen, coords, columns, inverse, near_own, near_par,
     ext_rows, exchanged, kern_own, kern_par, kern_ext, send_own, send_ext, got_own, got_ext,
     weighted, tiles, to_mate, from_mate, to_owner, from_owner, line,
     local_sem, occ_send, occ_recv, mate_send, mate_recv,
@@ -50,7 +50,8 @@
     side = 1 - 2 * lax.rem(lax.div(b, 2), 2)
     same, ahead, behind, diagonal = side, 2 * side, -2 * side, -side
     has_ahead, has_behind = exists(ahead), exists(behind)
-    two_parts = ((0, SPLIT), (SPLIT, PANELS_DEV - SPLIT))
+    near_parts, far_parts = range(SPLIT), range(SPLIT, PANELS_DEV)
+    every = range(PANELS_DEV)
 
     def remote(src, dst, send, recv, to):
         return pltpu.make_async_remote_copy(
@@ -85,6 +86,7 @@
         pltpu.make_async_copy(centres_hbm.at[:, pl.ds(pl.multiple_of(b * points, 128), points)], coords.at[0, pl.ds(0, 3)], local_sem.at[2]),
         pltpu.make_async_copy(centres_hbm.at[:, pl.ds(pl.multiple_of(mate * points, 128), points)], coords.at[1, pl.ds(0, 3)], local_sem.at[3]),
         pltpu.make_async_copy(weights_hbm, line, local_sem.at[4]),
+        pltpu.make_async_copy(listed_hbm, listed, local_sem.at[6]),
     ]
     coords[...] = jnp.zeros_like(coords)
     for load in loads:
@@ -97,17 +99,15 @@
     pl.semaphore_wait(barrier, expected)
 
     def panel_slot(d, h):
-        start, size = two_parts[h]
-        return cand.at[pl.ds(PANELS_DEV * (4 + 2 * d + k) + start, size)]
+        return cand.at[pl.ds(PANELS_DEV * (4 + 2 * d + k) + h, 1)]
 
     def panel_copy(role, h):
-        start, size = two_parts[h]
-        mine = occ_hbm.at[pl.ds(start, size)]
+        mine = occ_hbm.at[pl.ds(h, 1)]
         src, to, dst = (
             (mine, same, -same),
             (mine, behind, ahead),
             (mine, ahead, behind),
-            (panel_slot(same, h), ahead, diagonal) if h == 0 else (panel_slot(ahead, h), same, same),
+            (panel_slot(same, h), ahead, diagonal) if h in near_parts else (panel_slot(ahead, h), same, same),
         )[role]
         return remote(src, panel_slot(dst, h), occ_send.at[role, h], occ_recv.at[role, h], at(c, pair(to)))
 
@@ -117,19 +117,21 @@
         slot = panel_slot(arrives_from[role], h)
         return remote(slot, slot, mate_send.at[role, h], mate_recv.at[role, h], at(c, mate))
 
-    panel_copy(0, 0).start()
+    for h in near_parts:
+        panel_copy(0, h).start()
 
     @pl.when(has_behind)
     def _():
-        panel_copy(1, 1).start()
-        panel_copy(1, 0).start()
+        for h in (*far_parts, *near_parts):
+            panel_copy(1, h).start()
 
     @pl.when(has_ahead)
     def _():
-        panel_copy(2, 1).start()
-        panel_copy(2, 0).start()
-
-    panel_copy(0, 1).start()
+        for h in (*far_parts, *near_parts):
+            panel_copy(2, h).start()
+
+    for h in far_parts:
+        panel_copy(0, h).start()
     whole_slot = cand.at[pl.ds(PANELS_DEV * (4 + k), PANELS_DEV)]
     panel_mate = remote(occ_hbm, whole_slot, mate_send.at[4, 0], mate_recv.at[4, 0], at(c, mate))
     panel_mate.start()
@@ -156,6 +158,122 @@
 
     first = (b - k - 4) * PANELS_DEV
 
+    def panel_here(role, h):
+        panel_copy(role, h).wait_recv()
+        panel_pass(role, h).start()
+
+    for h in near_parts:
+        panel_here(0, h)
+        pl.when(has_ahead)(panel_copy(3, h).start)
+
+    @pl.when(has_ahead)
+    def _():
+        for h in far_parts:
+            panel_here(1, h)
+            panel_copy(3, h).start()
+
+    @pl.when(has_behind)
+    def _():
+        for h in far_parts:
+            panel_here(2, h)
+
+    for h in far_parts:
+        panel_here(0, h)
+
+    @pl.when(has_ahead)
+    def _():
+        for h in near_parts:
+            panel_here(1, h)
+
+    @pl.when(has_behind)
+    def _():
+        for h in near_parts:
+            panel_here(2, h)
+        for h in every:
+            panel_here(3, h)
+
+    panel_mate.wait()
+    for h in every:
+        panel_pass(0, h).wait()
+        panel_copy(0, h).wait_send()
+
+    @pl.when(has_ahead)
+    def _():
+        for h in every:
+            panel_pass(1, h).wait()
+            panel_copy(2, h).wait_send()
+            panel_copy(3, h).wait_send()
+
+    @pl.when(has_behind)
+    def _():
+        for h in every:
+            panel_pass(2, h).wait()
+            panel_pass(3, h).wait()
+            panel_copy(1, h).wait_send()
+
+    def choose(s, carry):
+        chosen[pl.ds(pl.multiple_of(s * PANEL_ROWS, 128), PANEL_ROWS), :] = cand[jnp.clip(listed[0, s] - first, 0, 10 * PANELS_DEV - 1)]
+        return carry
+
+    lax.fori_loop(0, LISTED, choose, 0)
+
+    across = c + 1 - 2 * lax.rem(c, 2)
+    up = lax.rem(c + 2, nc)
+    down = lax.rem(c + nc - 2, nc)
+    far = lax.rem(c + 4, nc)
+
+    def other(slab):
+        return slab + 1 - 2 * lax.rem(slab, 2)
+
+    arrives = (down, up, across, far, other(down), other(up), other(far), c)
+    leaves = (
+        (c, up), (c, down), (c, across), None, (across, up), (across, down), (far, across),
+    )
+
+    def piece(buffer, slab, r):
+        return buffer.at[slab, pl.ds(r * part, part)]
+
+    def field_copy(kind, r):
+        slab, to = leaves[kind] or ((down, up) if r % 2 == 0 else (up, down))
+        return remote(
+            piece(near_own, slab, r), piece(near_own, slab, r),
+            field_send.at[kind, r], field_recv.at[kind, r], at(to, b),
+        )
+
+    def pass_copy(kind, r):
+        slab = arrives[kind]
+        return remote(
+            piece(near_own, slab, r), piece(near_par, slab, r),
+            pass_send.at[kind, r], pass_recv.at[kind, r], at(c, mate),
+        )
+
+    my_rows = pl.ds(pl.multiple_of(c * rows, 16), rows)
+
+    holders = (up, down, across, far, other(up), other(down), other(far), c)
+
+    def ext_copy(kind):
+        to = holders[kind]
+        to_rows = pl.ds(pl.multiple_of(to * rows, 16), rows)
+        return remote(near_own.at[c, to_rows], ext_rows.at[c], ext_send.at[kind], ext_recv.at[kind], at(to, outer))
+
+    def arrived(kind, r, forward=()):
+        field_copy(kind, r).wait_recv()
+        for onward in forward:
+            field_copy(onward, r).start()
+        pass_copy(kind, r).start()
+
+    for r in range(ROW_PARTS):
+        near_own[c, r * part : (r + 1) * part] = jnp.dot(
+            basis[r * part : (r + 1) * part], chosen[...], preferred_element_type=jnp.float32
+        ).astype(jnp.bfloat16)
+        for kind in (0, 1, 2):
+            if r >= 2:
+                field_copy(kind, r - 2).wait_send()
+            field_copy(kind, r).start()
+        pass_copy(7, r).start()
+    for kind in range(nc):
+        pl.when(inside)(ext_copy(kind).start)
+
     def invert(q, carry):
         slot = jnp.int32(LISTED)
         for s in range(LISTED):
@@ -165,106 +283,6 @@
 
     lax.fori_loop(0, 10 * PANELS_DEV, invert, 0)
     tiles[LISTED] = jnp.zeros_like(tiles[LISTED])
-
-    def panel_here(role, h):
-        panel_copy(role, h).wait_recv()
-        panel_pass(role, h).start()
-
-    panel_here(0, 0)
-
-    @pl.when(has_ahead)
-    def _():
-        panel_copy(3, 0).start()
-        panel_here(1, 1)
-        panel_copy(3, 1).start()
-
-    pl.when(has_behind)(lambda: panel_here(2, 1))
-    panel_here(0, 1)
-    pl.when(has_ahead)(lambda: panel_here(1, 0))
-
-    @pl.when(has_behind)
-    def _():
-        panel_here(2, 0)
-        panel_here(3, 0)
-        panel_here(3, 1)
-
-    panel_mate.wait()
-    for h in range(2):
-        panel_pass(0, h).wait()
-        panel_copy(0, h).wait_send()
-
-        @pl.when(has_ahead)
-        def _(h=h):
-            panel_pass(1, h).wait()
-            panel_copy(2, h).wait_send()
-            panel_copy(3, h).wait_send()
-
-        @pl.when(has_behind)
-        def _(h=h):
-            panel_pass(2, h).wait()
-            panel_pass(3, h).wait()
-            panel_copy(1, h).wait_send()
-
-    def choose(s, carry):
-        chosen[pl.ds(pl.multiple_of(s * PANEL_ROWS, 128), PANEL_ROWS), :] = cand[jnp.clip(listed[0, s] - first, 0, 10 * PANELS_DEV - 1)]
-        return carry
-
-    lax.fori_loop(0, LISTED, choose, 0)
-
-    across = c + 1 - 2 * lax.rem(c, 2)
-    up = lax.rem(c + 2, nc)
-    down = lax.rem(c + nc - 2, nc)
-    far = lax.rem(c + 4, nc)
-
-    def other(slab):
-        return slab + 1 - 2 * lax.rem(slab, 2)
-
-    arrives = (down, up, across, far, other(down), other(up), other(far), c)
-    leaves = (
-        (c, up), (c, down), (c, across), None, (across, up), (across, down), (far, across),
-    )
-
-    def piece(buffer, slab, r):
-        return buffer.at[slab, pl.ds(r * part, part)]
-
-    def field_copy(kind, r):
-        slab, to = leaves[kind] or ((down, up) if r % 2 == 0 else (up, down))
-        return remote(
-            piece(near_own, slab, r), piece(near_own, slab, r),
-            field_send.at[kind, r], field_recv.at[kind, r], at(to, b),
-        )
-
-    def pass_copy(kind, r):
-        slab = arrives[kind]
-        return remote(
-            piece(near_own, slab, r), piece(near_par, slab, r),
-            pass_send.at[kind, r], pass_recv.at[kind, r], at(c, mate),
-        )
-
-    my_rows = pl.ds(pl.multiple_of(c * rows, 16), rows)
-
-    holders = (up, down, across, far, other(up), other(down), other(far), c)
-
-    def ext_copy(kind):
-        to = holders[kind]
-        to_rows = pl.ds(pl.multiple_of(to * rows, 16), rows)
-        return remote(near_own.at[c, to_rows], ext_rows.at[c], ext_send.at[kind], ext_recv.at[kind], at(to, outer))
-
-    def arrived(kind, r, forward=()):
-        field_copy(kind, r).wait_recv()
-        for onward in forward:
-            field_copy(onward, r).start()
-        pass_copy(kind, r).start()
-
-    for r in range(ROW_PARTS):
-        near_own[c, r * part : (r + 1) * part] = jnp.dot(
-            basis[r * part : (r + 1) * part], chosen[...], preferred_element_type=jnp.float32
-        ).astype(jnp.bfloat16)
-        for kind in (2, 0, 1):
-            field_copy(kind, r).start()
-        pass_copy(7, r).start()
-    for kind in range(nc):
-        pl.when(inside)(ext_copy(kind).start)
 
     parts = range(ROW_PARTS)
     for r in parts:
@@ -346,7 +364,8 @@
     lax.fori_loop(0, nc, finish, 0)
     for kind in range(len(leaves)):
         for r in range(ROW_PARTS):
-            field_copy(kind, r).wait_send()
+            if kind > 2 or r >= ROW_PARTS - 2:
+                field_copy(kind, r).wait_send()
 
     for i in range(nc):
         total = got_own[i].astype(jnp.float32)
@@ -371,26 +390,23 @@
         return remote(to_mate.at[i], from_mate.at[i], comb_send.at[i], comb_recv.at[i], at(c, mate))
 
     def part_of(buffer, i, h):
-        start, size = two_parts[h]
-        return buffer.at[i, pl.ds(start, size)]
+        return buffer.at[i, pl.ds(h, 1)]
 
     def final_copy(i, h):
-        to = (behind, same)[h] if i == DIAGONAL else order[i]
+        to = (behind if h in near_parts else same) if i == DIAGONAL else order[i]
         return remote(
             part_of(to_owner, i, h), part_of(from_owner, i, h), final_send.at[i, h], final_recv.at[i, h], at(c, pair(to))
         )
 
     def combine(i, h, merge=False):
-        start, size = two_parts[h]
-        for j in range(start, start + size):
-            total = tiles[inverse[PANELS_DEV * (4 + 2 * order[i] + k) + j]] + from_mate[i, j].astype(jnp.float32)
-            if merge:
-                term = from_owner[DIAGONAL, j].astype(jnp.float32)
-                total = total + jnp.where(has_ahead, term, jnp.zeros_like(term))
-            if i == HERE:
-                out_ref[j] = total
-            else:
-                to_owner[i, j] = total.astype(jnp.bfloat16)
+        total = tiles[inverse[PANELS_DEV * (4 + 2 * order[i] + k) + h]] + from_mate[i, h].astype(jnp.float32)
+        if merge:
+            term = from_owner[DIAGONAL, h].astype(jnp.float32)
+            total = total + jnp.where(has_ahead, term, jnp.zeros_like(term))
+        if i == HERE:
+            out_ref[h] = total
+        else:
+            to_owner[i, h] = total.astype(jnp.bfloat16)
 
     for i, d in enumerate(order):
         for j in range(PANELS_DEV):
@@ -398,34 +414,38 @@
         comb_copy(i).start()
 
     comb_copy(DIAGONAL).wait()
-    for h in (1, 0):
+    for h in (3, 0, 4, 1, 2):
         combine(DIAGONAL, h)
         pl.when(has_behind)(final_copy(DIAGONAL, h).start)
     comb_copy(SAME).wait()
-    combine(SAME, 1)
-    final_copy(SAME, 1).start()
+    for h in far_parts:
+        combine(SAME, h)
+        final_copy(SAME, h).start()
     comb_copy(AHEAD).wait()
-    combine(AHEAD, 0)
-    pl.when(has_ahead)(final_copy(AHEAD, 0).start)
+    for h in near_parts:
+        combine(AHEAD, h)
+        pl.when(has_ahead)(final_copy(AHEAD, h).start)
     comb_copy(BEHIND).wait()
-    for h in range(2):
+    for h in every:
         combine(BEHIND, h)
         pl.when(has_behind)(final_copy(BEHIND, h).start)
     comb_copy(HERE).wait()
-    for h in range(2):
+    for h in every:
         combine(HERE, h)
-    pl.when(has_ahead)(final_copy(DIAGONAL, 0).wait_recv)
-    combine(SAME, 0, merge=True)
-    final_copy(SAME, 0).start()
+    for h in near_parts:
+        pl.when(has_ahead)(final_copy(DIAGONAL, h).wait_recv)
+        combine(SAME, h, merge=True)
+        final_copy(SAME, h).start()
 
     @pl.when(has_ahead)
     def _():
-        final_copy(DIAGONAL, 1).wait_recv()
-        combine(AHEAD, 1, merge=True)
-        final_copy(AHEAD, 1).start()
+        for h in far_parts:
+            final_copy(DIAGONAL, h).wait_recv()
+            combine(AHEAD, h, merge=True)
+            final_copy(AHEAD, h).start()
 
     for i, sent in ((BEHIND, has_ahead), (SAME, None), (AHEAD, has_behind)):
-        for h in range(2):
+        for h in every:
             if sent is None:
                 final_copy(i, h).wait_recv()
             else:
@@ -433,9 +453,11 @@
         for j in range(PANELS_DEV):
             term = from_owner[i, j].astype(jnp.float32)
             out_ref[j] += term if sent is None else jnp.where(sent, term, jnp.zeros_like(term))
-    for j in range(PANELS_DEV):
+    results = [pltpu.make_async_copy(out_ref.at[j], out_hbm.at[j], local_sem.at[j]) for j in range(PANELS_DEV)]
+    for j, result in enumerate(results):
         out_ref[j] = out_ref[j].T
-    for h in range(2):
+        result.start()
+    for h in every:
         final_copy(SAME, h).wait_send()
         pl.when(has_ahead)(final_copy(AHEAD, h).wait_send)
 
@@ -443,6 +465,9 @@
         def _(h=h):
             final_copy(DIAGONAL, h).wait_send()
             final_copy(BEHIND, h).wait_send()
+
+    for result in results:
+        result.wait()
 
 
 def solution(mesh):
@@ -459,9 +484,11 @@
         out = pl.pallas_call(
             functools.partial(fused, nc, ng, nc * width),
             out_shape=jax.ShapeDtypeStruct((PANELS_DEV, *panel), f32),
-            in_specs=[anywhere, anywhere, pl.BlockSpec(memory_space=pltpu.SMEM), anywhere, anywhere],
-            out_specs=pl.BlockSpec(memory_space=pltpu.VMEM),
+            in_specs=[anywhere] * 5,
+            out_specs=anywhere,
             scratch_shapes=[
+                pltpu.SMEM((1, LISTED), jnp.int32),
+                pltpu.VMEM((PANELS_DEV, *panel), f32),
                 pltpu.VMEM((points, functions), bf16),
                 pltpu.VMEM((10 * PANELS_DEV, *panel), bf16),
                 pltpu.VMEM((functions, width), bf16),
@@ -486,13 +513,13 @@
                 pltpu.VMEM((4, PANELS_DEV, *panel), bf16),
                 pltpu.VMEM((4, PANELS_DEV, *panel), bf16),
                 pltpu.VMEM((points,), f32),
-                dma((6,)),
-                dma((4, 2)), dma((4, 2)), dma((5, 2)), dma((5, 2)),
+                dma((8,)),
+                dma((4, PANELS_DEV)), dma((4, PANELS_DEV)), dma((5, PANELS_DEV)), dma((5, PANELS_DEV)),
                 dma((nc, ROW_PARTS)), dma((nc, ROW_PARTS)),
                 dma((nc, ROW_PARTS)), dma((nc, ROW_PARTS)),
                 dma((nc,)), dma((nc,)),
                 dma((nc,)), dma((nc,)), dma((nc,)), dma((nc,)),
-                dma((5,)), dma((5,)), dma((4, 2)), dma((4, 2)),
+                dma((5,)), dma((5,)), dma((4, PANELS_DEV)), dma((4, PANELS_DEV)),
             ],
             compiler_params=pltpu.CompilerParams(
                 collective_id=0, has_side_effects=True, vmem_limit_bytes=56 * 2**20

time: 57.4 us -> 56.6 us (0.986)
  Pallas kernels: 55.6 us -> 54.7 us
    pallas_call x1, Pallas kernels: 55.6 us -> 54.7 us  [shards(): pl.pallas_call(functools.partial(fused, nc, ng, nc * width), out_shape=ja...]
where the time goes in v7:
time: 56.6 us; the launch traced here: 56.4 us
  Pallas kernels  54.7 us (97%)
  local copies, waits for them, and re-layouts  1.72 us (3%)
    pallas_call x1, Pallas kernels, shards(): pl.pallas_call(functools.partial(fused, nc, ng, nc * width), out_shape=ja...  54.7 us
    unnamed x1, local copies, waits for them, and re-layouts  1.72 us

profile of v7, /device:TPU:96, one launch (start us, length us, event | category | flops | bytes accessed | tf_op | source)
XLA Modules:
  0.0 56.4 jit_solution(5970740954608974474)
XLA Ops:
  0.0 54.7 %shard_map.55 = f32[5,128,128]{2,1,0:T(8,128)} custom-call(bf16[640,2688]{1,0:T(8,128)(2,1)} %basis_hbm.1, bf16[5,128,128]{2,1,0:T(8,128)(2,1)} %bitcast.3, s32[1,21]{1,0:T(1,128)} %listed_hbm.1, f32[3,40960]{1,0:T(4,128)} %centres_hbm.1, f32[640]{0:T(1024)} %weights_hbm.1), custom_call_target="tpu_custom_call" | custom-call | tf_op jit(solution)/shard_map/pallas_call | solution.py:484
  54.7 1.7 %copy.7 = f32[640,128]{1,0:T(8,128)} copy(f32[640,128]{1,0:T(8,128)} %bitcast.2) | data formatting | bytes 655360

commit v8 on v7

--- a/solution.py
+++ b/solution.py
@@ -303,8 +303,9 @@
     def beside(ref, slabs, at_rows=slice(None)):
         return jnp.concatenate([ref[slab, at_rows, :] for slab in slabs], axis=1)
 
-    def two(i):
-        return (2 * i, 2 * i + 1)
+    def two(n):
+        place = lax.rem(lax.div(c, 2) + jnp.where(n < 2, n + 2, 3 - n), nc // 2)
+        return (2 * place, 2 * place + 1)
 
     @pl.when(inside)
     def _():

time: 56.6 us -> 56.6 us (level)
  no operation moved by 1% of the time
where the time goes in v8:
time: 56.6 us; the launch traced here: 56.5 us
  Pallas kernels  54.7 us (97%)
  local copies, waits for them, and re-layouts  1.72 us (3%)
    pallas_call x1, Pallas kernels, shards(): pl.pallas_call(functools.partial(fused, nc, ng, nc * width), out_shape=ja...  54.7 us
    unnamed x1, local copies, waits for them, and re-layouts  1.72 us

profile of v8, /device:TPU:96, one launch (start us, length us, event | category | flops | bytes accessed | tf_op | source)
XLA Modules:
  0.0 56.5 jit_solution(6261240569681259419)
XLA Ops:
  0.0 54.7 %shard_map.55 = f32[5,128,128]{2,1,0:T(8,128)} custom-call(bf16[640,2688]{1,0:T(8,128)(2,1)} %basis_hbm.1, bf16[5,128,128]{2,1,0:T(8,128)(2,1)} %bitcast.3, s32[1,21]{1,0:T(1,128)} %listed_hbm.1, f32[3,40960]{1,0:T(4,128)} %centres_hbm.1, f32[640]{0:T(1024)} %weights_hbm.1), custom_call_target="tpu_custom_call" | custom-call | tf_op jit(solution)/shard_map/pallas_call | solution.py:485
  54.7 1.7 %copy.7 = f32[640,128]{1,0:T(8,128)} copy(f32[640,128]{1,0:T(8,128)} %bitcast.2) | data formatting | bytes 655360

commit v9 on v8

--- a/solution.py
+++ b/solution.py
@@ -11,7 +11,6 @@
 PANEL_ROWS = 128
 PANELS_DEV = 5
 LISTED = 21
-PAIRS = (-2, -1, 1, 2)
 ROW_PARTS = 4
 SPLIT = 3
 MESH = pl.DeviceIdType.MESH
@@ -63,13 +62,14 @@
 
     barrier = pltpu.get_barrier_semaphore()
     pl.semaphore_signal(barrier, inc=1, device_id=at(c, mate), device_id_type=MESH)
-    expected = jnp.int32(nc)
-    for d in PAIRS:
-        @pl.when(exists(d))
+    pl.semaphore_signal(barrier, inc=1, device_id=at(c, pair(same)), device_id_type=MESH)
+    expected = jnp.int32(nc + 1)
+    for d, there in ((ahead, has_ahead), (behind, has_behind)):
+        @pl.when(there)
         def _(d=d):
             pl.semaphore_signal(barrier, inc=1, device_id=at(c, pair(d)), device_id_type=MESH)
 
-        expected += exists(d).astype(jnp.int32)
+        expected += there.astype(jnp.int32)
     for j in range(1, nc):
         pl.semaphore_signal(barrier, inc=1, device_id=at(coef_of(j), b), device_id_type=MESH)
 

time: 56.6 us -> 56.3 us (level)
  the two profiles are of different devices: /device:TPU:96 before, /device:TPU:1 now
where the time goes in v9:
time: 56.3 us; the launch traced here: 56.2 us
  Pallas kernels  54.5 us (97%)
  local copies, waits for them, and re-layouts  1.72 us (3%)
    pallas_call x1, Pallas kernels, shards(): pl.pallas_call(functools.partial(fused, nc, ng, nc * width), out_shape=ja...  54.5 us
    unnamed x1, local copies, waits for them, and re-layouts  1.72 us

profile of v9, /device:TPU:1, one launch (start us, length us, event | category | flops | bytes accessed | tf_op | source)
XLA Modules:
  0.0 56.2 jit_solution(7455705316248096905)
XLA Ops:
  0.0 54.5 %shard_map.55 = f32[5,128,128]{2,1,0:T(8,128)} custom-call(bf16[640,2688]{1,0:T(8,128)(2,1)} %basis_hbm.1, bf16[5,128,128]{2,1,0:T(8,128)(2,1)} %bitcast.3, s32[1,21]{1,0:T(1,128)} %listed_hbm.1, f32[3,40960]{1,0:T(4,128)} %centres_hbm.1, f32[640]{0:T(1024)} %weights_hbm.1), custom_call_target="tpu_custom_call" | custom-call | tf_op jit(solution)/shard_map/pallas_call | solution.py:485
  54.5 1.7 %copy.7 = f32[640,128]{1,0:T(8,128)} copy(f32[640,128]{1,0:T(8,128)} %bitcast.2) | data formatting | bytes 655360
